TPU v7x, 768 devices: a whole 4x8x12 slice. The times are simulated.
768 devices in a mesh: occ: 8 (over x, core), vir: 96 (over y, z).
Axes of the slice: x: 4, y: 8, z: 12, core: 2. Of those that a mesh axis runs over, the one named last changes fastest.
Arguments:
- amplitudes: bfloat16 [4096, 3072], P('occ', 'vir'), may hold values from -6 to 6
- integrals: bfloat16 [3072, 98304], P('occ', 'vir'), may hold values from -0.109375 to 0.109375
- amp_mask: int32 [64, 48], P('occ'), may hold values 0 or 1
- int_mask: int32 [48, 1536], P('occ', 'vir'), may hold values 0 or 1
Outputs:
- ladder: bfloat16 [4096, 98304], P('occ', 'vir')
All inputs are finite; a program needn't handle non-finite values. No bound on the sum of `amp_mask` or of `int_mask` on one device may be relied on, other than what follows from the above.
Results may differ from a plain program's by a relative error of at most 0.001.
Values may be sent and summed in bfloat16 or wider, within the bound.
No kernel may reach another device: no remote copies, remote signals or barrier semaphores. Data moves between devices by JAX's collectives and lax.ppermute only.
A program may use at most 32 MiB of HBM per device.

v0:
```python
import jax
import jax.numpy as jnp
from jax import lax
from jax.sharding import PartitionSpec as P

TILE = 64


def on_device(amplitudes, integrals, amp_mask, int_mask):
    cd_local = amplitudes.shape[1]
    vir_index = lax.axis_index("vir")
    columns = vir_index * cd_local + jnp.arange(cd_local, dtype=jnp.int32)
    tile_index = columns // TILE
    onehot = (
        jnp.arange(amp_mask.shape[1], dtype=jnp.int32)[:, None] == tile_index[None, :]
    ).astype(jnp.float32)
    col_mask = jnp.dot(amp_mask.astype(jnp.float32), onehot)
    row_mask = jnp.repeat(col_mask, TILE, axis=0).astype(jnp.bfloat16)
    masked_amps = amplitudes * row_mask
    tile_mask = jnp.repeat(jnp.repeat(int_mask, TILE, axis=0), TILE, axis=1).astype(jnp.bfloat16)
    masked_ints = integrals * tile_mask
    gathered_amps = lax.all_gather(masked_amps, "vir", axis=1, tiled=True)
    gathered_ints = lax.all_gather(masked_ints, "occ", axis=0, tiled=True)
    ladder = jnp.dot(gathered_amps, gathered_ints, preferred_element_type=jnp.float32)
    return ladder.astype(jnp.bfloat16)


def solution(mesh):
    return jax.shard_map(
        on_device,
        mesh=mesh,
        in_specs=(P("occ", "vir"), P("occ", "vir"), P("occ", None), P("occ", "vir")),
        out_specs=P("occ", "vir"),
        check_vma=False,
    )
```

profile of v0, /device:TPU:1, one launch (start us, length us, event | category | flops | bytes accessed | tf_op | source)
XLA Modules:
  0.0 206.7 jit_solution(7133779919008996607)
XLA Ops:
  6.5 0.0 all-gather.3.cloned.1.call-start
  6.5 0.8 fusion
  7.4 0.1 copy.9
  7.5 0.1 broadcast_in_dim.11
  7.6 0.1 convert_element_type.31
  7.7 1.4 mul.10
  9.1 0.0 all-gather.3.cloned.1.call-update
  9.1 0.0 all-gather.5.cloned.1.call-start
  9.1 0.7 convert_element_type.32
  9.8 0.1 copy.10
  9.9 0.1 broadcast_in_dim.12
  10.0 0.1 convert_element_type.33
  10.1 1.5 copy.11
  11.6 1.0 bitcast_multiply_fusion
  12.6 0.0 all-gather.5.cloned.1.call-update
  12.6 125.4 %all-gather.3.cloned.1.call-done = bf16[512,3072]{0,1:T(8,128)(2,1)} async-done(((bf16[512,32]{0,1:T(8,128)(2,1)}), bf16[512,3072]{0,1:T(8,128)(2,1)}) %all-gather.3.cloned.1.call-update) | async-done | bytes 3145744 | tf_op jit(solution)/shard_map/all_gather | solution.py:22
  138.0 53.7 %all-gather.5.cloned.1.call-done = bf16[3072,1024]{0,1:T(8,128)(2,1)} async-done(((bf16[384,1024]{0,1:T(8,128)(2,1)}), bf16[3072,1024]{0,1:T(8,128)(2,1)}) %all-gather.5.cloned.1.call-update) | async-done | bytes 6291472 | tf_op jit(solution)/shard_map/all_gather | solution.py:23
  191.7 8.2 %convolution_convert_fusion = bf16[512,1024]{1,0:T(8,128)(2,1)} fusion(bf16[512,3072]{0,1:T(8,128)(2,1)} %all-gather.3.cloned.1.call-done, bf16[3072,1024]{0,1:T(8,128)(2,1)} %all-gather.5.cloned.1.call-done), kind=kOutput, calls=%fused_computation | convolution fusion | flops 3221749760 | bytes 10485760 | tf_op jit(solution)/shard_map/dot_general | solution.py:24
  (1 shorter events, 0.0 us)
Async XLA Ops:
  6.5 131.4 %all-gather.3.cloned.1.call-start = ((), (), s32[]{:S(2)}) async-start(), calls=%async_computation | async-start | bytes 3178496 | tf_op jit(solution)/shard_map/all_gather | solution.py:22
  9.1 182.6 %all-gather.5.cloned.1.call-start = ((), (), s32[]{:S(2)}) async-start(), calls=%async_computation.1 | async-start | bytes 7077888 | tf_op jit(solution)/shard_map/all_gather | solution.py:23
Sparse Core Ops, SparseCore 0:
  11.1 126.8 all-gather.2
  140.4 51.2 all-gather.4
where the time goes:
time: 207 us
  waiting for transfers between devices  179 us (86%)
  between operations  13.4 us (6%)
  matrix products  8.99 us (4%)
  other arithmetic  3.05 us (1%)
  local copies, waits for them, and re-layouts  2.1 us (1%)
    all_gather x1, waiting for transfers between devices, on_device(): gathered_amps = lax.all_gather(masked_amps, 'vir', axis=1, tiled=True)  125 us
    all_gather x1, waiting for transfers between devices, on_device(): gathered_ints = lax.all_gather(masked_ints, 'occ', axis=0, tiled=True)  53.7 us
    dot_general x1, matrix products, on_device(): jnp.dot(gathered_amps, gathered_ints, preferred_element_type=jnp.float32)  8.18 us
  transfers between devices with their start and end apart: 2, of which 2 were waited for; matrix products, arithmetic and copies ran while one was open for 2% of the time, Pallas kernels for 0%

commit v1 on v0

v1 whole, which is shorter than its diff:
```python
import jax
import jax.numpy as jnp
from jax import lax
from jax.experimental import pallas as pl
from jax.experimental.pallas import tpu as pltpu
from jax.sharding import PartitionSpec as P

TILE = 64
Y, Z = 8, 12
FAR, NEAR = 2, 4
COLS = 256


def vir(y, z):
    return (y % Y) * Z + z % Z


Z_GROUPS = [[vir(y, z) for z in range(Z)] for y in range(Y)]
FAR_GROUPS = [[vir(near + NEAR * k, z) for k in range(FAR)] for near in range(NEAR) for z in range(Z)]


def spread(block, axis, groups):
    copies = jnp.broadcast_to(block[None], (len(groups[0]),) + block.shape)
    return lax.all_to_all(copies, axis, 0, 0, axis_index_groups=groups)


def shift_y(block, step):
    return lax.ppermute(block, "vir", [(vir(y, z), vir(y + step, z)) for y in range(Y) for z in range(Z)])


def screen_kernel(mask_ref, block_ref, out_ref):
    depth, cols = block_ref.shape
    tiles, tile_cols = mask_ref.shape
    across = lax.broadcasted_iota(jnp.int32, (tile_cols, cols), 1) // TILE
    spread_to = (across == lax.broadcasted_iota(jnp.int32, (tile_cols, cols), 0)).astype(jnp.float32)
    rows = jnp.dot(mask_ref[...].astype(jnp.float32), spread_to, preferred_element_type=jnp.float32).astype(jnp.bfloat16)
    for t in range(tiles):
        part = slice(t * TILE, (t + 1) * TILE)
        out_ref[part, :] = block_ref[part, :] * rows[t : t + 1, :]


def screen(block, mask):
    return pl.pallas_call(
        screen_kernel,
        out_shape=jax.ShapeDtypeStruct(block.shape, block.dtype),
        compiler_params=pltpu.CompilerParams(vmem_limit_bytes=40 * 1024 * 1024),
        cost_estimate=pl.CostEstimate(flops=block.size, bytes_accessed=4 * block.size, transcendentals=0),
    )(mask, block)


def product_kernel(offsets, has_acc, where, mask_ref, *refs):
    n = len(offsets)
    near = where[0]
    t_refs, refs = refs[: 2 * n], refs[2 * n :]
    v_refs, refs = refs[:n], refs[n:]
    acc_ref, refs = (refs[0], refs[1:]) if has_acc else (None, refs)
    out_ref, lhs, row_mask = refs
    some, far, r, rows = t_refs[0].shape
    zs = 2 * some
    depth = zs * far * r
    per = TILE // r

    @pl.when(pl.program_id(0) == 0)
    def _():
        tiles = mask_ref.shape[0]
        tile_of = lax.broadcasted_iota(jnp.int32, (tiles, rows), 1) // TILE
        spread_to = (tile_of == lax.broadcasted_iota(jnp.int32, (tiles, rows), 0)).astype(jnp.float32)
        row_mask[...] = lax.dot_general(
            mask_ref[...].astype(jnp.float32), spread_to, (((0,), (0,)), ((), ())), preferred_element_type=jnp.float32
        )
        for q, off in enumerate(offsets):
            residue = lax.rem(near + off, NEAR)
            blocks = []
            for f in range(far):
                for z in range(zs):
                    tile = (residue + NEAR * f) * (zs // per) + z // per
                    mask = row_mask[pl.ds(tile, 1), :].astype(jnp.bfloat16)
                    blocks.append(t_refs[2 * q + z // some][z % some, f] * mask)
            lhs[:, q * depth : (q + 1) * depth] = jnp.concatenate(blocks, axis=0).T

    rhs = jnp.concatenate([v[...].reshape(depth, -1) for v in v_refs], axis=0)
    total = jnp.dot(lhs[...], rhs, preferred_element_type=jnp.float32)
    if has_acc:
        total = total + acc_ref[...]
    out_ref[...] = total.astype(out_ref.dtype)


def product(where, offsets, ts, amp_mask, v, acc, dtype):
    n = len(offsets)
    some, far, r, rows = ts[0].shape
    cols = v.shape[-1]
    depth = 2 * some * far * r

    def strip(off):
        return pl.BlockSpec((far, 1, v.shape[2], COLS), lambda i, w: (0, lax.rem(w[0] + off, NEAR), 0, i))

    in_specs = [pl.BlockSpec(amp_mask.shape, lambda i, w: (0, 0))]
    in_specs += [pl.BlockSpec((some, far, r, rows), lambda i, w: (0, 0, 0, 0)) for _ in ts]
    in_specs += [strip(off) for off in offsets]
    operands = [amp_mask] + list(ts) + [v] * n
    if acc is not None:
        in_specs.append(pl.BlockSpec((rows, COLS), lambda i, w: (0, i)))
        operands.append(acc)
    return pl.pallas_call(
        lambda *refs: product_kernel(offsets, acc is not None, *refs),
        grid_spec=pltpu.PrefetchScalarGridSpec(
            num_scalar_prefetch=1,
            grid=(cols // COLS,),
            in_specs=in_specs,
            out_specs=pl.BlockSpec((rows, COLS), lambda i, w: (0, i)),
            scratch_shapes=[
                pltpu.VMEM((rows, n * depth), jnp.bfloat16),
                pltpu.VMEM((amp_mask.shape[1], rows), jnp.float32),
            ],
        ),
        out_shape=jax.ShapeDtypeStruct((rows, cols), dtype),
        compiler_params=pltpu.CompilerParams(vmem_limit_bytes=40 * 1024 * 1024),
        cost_estimate=pl.CostEstimate(
            flops=2 * rows * cols * n * depth,
            bytes_accessed=2 * n * depth * (rows + cols) + 4 * rows * cols,
            transcendentals=0,
        ),
    )(where, *operands)


def on_device(amplitudes, integrals, amp_mask, int_mask):
    depth, cols = integrals.shape
    near = lax.rem(lax.axis_index("vir") // Z, NEAR)
    where = near[None].astype(jnp.int32)

    pair = spread(amplitudes.T, "vir", FAR_GROUPS)
    pair, integrals = lax.optimization_barrier((pair, integrals))
    v = lax.all_gather(screen(integrals, int_mask), "occ", axis=0)
    w = lax.all_gather(pair, "vir", axis=0, axis_index_groups=Z_GROUPS)
    w_a, w_b = w[: Z // 2], w[Z // 2 :]
    below_a = shift_y(w_a, 1)
    above_b = shift_y(w_b, -1)
    below_b = shift_y(w_b, 1)
    above_a = shift_y(w_a, -1)
    two_a = shift_y(below_a, 1)
    two_b = shift_y(above_b, -1)

    v = v.reshape(FAR, NEAR, depth, cols)
    acc = product(where, (0,), (w_a, w_b), amp_mask, v, None, jnp.float32)
    acc = product(where, (1, 3), (above_a, above_b, below_a, below_b), amp_mask, v, acc, jnp.float32)
    return product(where, (2,), (two_a, two_b), amp_mask, v, acc, jnp.bfloat16)


def solution(mesh):
    return jax.shard_map(
        on_device,
        mesh=mesh,
        in_specs=(P("occ", "vir"), P("occ", "vir"), P("occ", None), P("occ", "vir")),
        out_specs=P("occ", "vir"),
        check_vma=False,
    )
```

time: 207 us -> 103 us (0.50)
  the two profiles are of different devices: /device:TPU:1 before, /device:TPU:2 now
where the time goes in v1:
time: 103 us
  blocking collectives  51.5 us (50%)
  starting transfers between devices  20 us (19%)
  between operations  13.6 us (13%)
  Pallas kernels  10.8 us (10%)
  local copies, waits for them, and re-layouts  5.78 us (6%)
    all_gather x1, blocking collectives, on_device(): w = lax.all_gather(pair, 'vir', axis=0, axis_index_groups=Z_GROUPS)  36.6 us
    ppermute x6, starting transfers between devices, shift_y(): lax.ppermute(block, 'vir', [(vir(y, z), vir(y + step, z)) for y in range(...  20 us
    all_to_all x1, blocking collectives, spread(): return lax.all_to_all(copies, axis, 0, 0, axis_index_groups=groups)  14.9 us
    pallas_call x3, Pallas kernels, product(): pl.pallas_call(lambda *refs: product_kernel(offsets, acc is not None, *re...  9.76 us
    unnamed x10, local copies, waits for them, and re-layouts  4.96 us
  transfers between devices with their start and end apart: 7, of which 1 were waited for; matrix products, arithmetic and copies ran while one was open for 0% of the time, Pallas kernels for 6%

profile of v1, /device:TPU:2, one launch (start us, length us, event | category | flops | bytes accessed | tf_op | source)
XLA Modules:
  0.0 102.7 jit_solution(15320196263415086950)
XLA Ops:
  6.5 0.0 all-gather.4.cloned.1.call-start
  6.5 0.8 broadcast_in_dim.10
  7.3 14.9 %all_to_all.5 = bf16[2,32,512]{2,1,0:T(8,128)(2,1)S(1)} all-to-all(bf16[2,32,512]{2,1,0:T(8,128)(2,1)S(1)} %broadcast_in_dim.10), channel_id=1, replica_groups={{0,48},{1,49},{2,50},{3,51},{4,52},{5,53},{6,54},{7,55},{8,56},{9,57},{..., dimensions={0} | all-to-all | bytes 131072 | tf_op jit(solution)/shard_map/all_to_all | solution.py:24
  22.2 0.0 copy-start.2
  22.2 1.1 %copy-done.2 = bf16[384,1024]{1,0:T(8,128)(2,1)S(1)} copy-done((bf16[384,1024]{1,0:T(8,128)(2,1)S(1)}, bf16[384,1024]{1,0:T(8,128)(2,1)}, u32[]{:S(2)}) %copy-start.2) | copy-done | bytes 786456
  23.3 0.0 copy-start.4
  23.3 0.7 copy-done.4
  24.0 0.0 copy-start.3
  24.0 1.1 %shard_map.46 = bf16[384,1024]{1,0:T(8,128)(2,1)} custom-call(s32[6,16]{1,0:T(8,128)S(1)} %copy-done.4, bf16[384,1024]{1,0:T(8,128)(2,1)S(1)} %copy-done.2), custom_call_target="tpu_custom_call" | custom-call | flops 393216 | bytes 1572864 | tf_op jit(solution)/shard_map/pallas_call | solution.py:43
  25.1 0.0 all-gather.4.cloned.1.call-update
  25.1 36.6 %all-gather = bf16[24,32,512]{2,1,0:T(8,128)(2,1)S(1)} all-gather(bf16[2,32,512]{2,1,0:T(8,128)(2,1)S(1)} %all_to_all.5), channel_id=2, replica_groups={{0,1,2,3,4,5,6,7,8,9,10,11},{12,13,14,15,16,17,18,19,20,21,22,23},{24,2..., dimensions={0}, use_global_device_ids=true | all-gather | bytes 851968 | tf_op jit(solution)/shard_map/all_gather | solution.py:134
  61.8 0.1 fusion
  61.9 2.8 %collective-permute-start = (bf16[6,2,32,512]{3,2,1,0:T(8,128)(2,1)S(1)}, bf16[6,2,32,512]{3,2,1,0:T(8,128)(2,1)S(1)}, u32[]{:S(2)}, u32[]{:S(2)}) collective-permute-start(bf16[6,2,32,512]{3,2,1,0:T(8,128)(2,1)S(1)} %bitcast.12), channel_id=1, source_target_pairs={{0,12},{1,13},{2,14},{3,15},{4,16},{5,17},{6,18},{7,19},{8,20},{9,... | collective-permute-start | bytes 1179656 | tf_op jit(solution)/shard_map/ppermute | solution.py:28
  64.7 4.2 %collective-permute-start.2 = (bf16[6,2,32,512]{3,2,1,0:T(8,128)(2,1)S(1)}, bf16[6,2,32,512]{3,2,1,0:T(8,128)(2,1)S(1)}, u32[]{:S(2)}, u32[]{:S(2)}) collective-permute-start(bf16[6,2,32,512]{3,2,1,0:T(8,128)(2,1)S(1)} %bitcast.9), channel_id=1, source_target_pairs={{0,84},{1,85},{2,86},{3,87},{4,88},{5,89},{6,90},{7,91},{8,92},{9,... | collective-permute-start | bytes 1179656 | tf_op jit(solution)/shard_map/ppermute | solution.py:28
  68.9 1.9 %collective-permute-start.4 = (bf16[6,2,32,512]{3,2,1,0:T(8,128)(2,1)S(1)}, bf16[6,2,32,512]{3,2,1,0:T(8,128)(2,1)S(1)}, u32[]{:S(2)}, u32[]{:S(2)}) collective-permute-start(bf16[6,2,32,512]{3,2,1,0:T(8,128)(2,1)S(1)} %bitcast.13), channel_id=1, source_target_pairs={{0,84},{1,85},{2,86},{3,87},{4,88},{5,89},{6,90},{7,91},{8,92},{9,... | collective-permute-start | bytes 1179656 | tf_op jit(solution)/shard_map/ppermute | solution.py:28
  70.9 3.9 %collective-permute-start.5 = (bf16[6,2,32,512]{3,2,1,0:T(8,128)(2,1)S(1)}, bf16[6,2,32,512]{3,2,1,0:T(8,128)(2,1)S(1)}, u32[]{:S(2)}, u32[]{:S(2)}) collective-permute-start(bf16[6,2,32,512]{3,2,1,0:T(8,128)(2,1)S(1)} %bitcast.10), channel_id=1, source_target_pairs={{0,12},{1,13},{2,14},{3,15},{4,16},{5,17},{6,18},{7,19},{8,20},{9,... | collective-permute-start | bytes 1179656 | tf_op jit(solution)/shard_map/ppermute | solution.py:28
  74.8 1.0 collective-permute-done.refs_4_
  75.8 1.9 %collective-permute-start.1 = (bf16[6,2,32,512]{3,2,1,0:T(8,128)(2,1)S(1)}, bf16[6,2,32,512]{3,2,1,0:T(8,128)(2,1)S(1)}, u32[]{:S(2)}, u32[]{:S(2)}) collective-permute-start(bf16[6,2,32,512]{3,2,1,0:T(8,128)(2,1)S(1)} %collective-permute-done.refs_4_), channel_id=1, source_target_pairs={{0,12},{1,13},{2,14},{3,15},{4,16},{5,17},{6,18},{7,19},{8,20},{9,... | collective-permute-start | bytes 1179656 | tf_op jit(solution)/shard_map/ppermute | solution.py:28
  77.7 0.0 collective-permute-done.2.refs_3_
  77.7 5.1 %collective-permute-start.3 = (bf16[6,2,32,512]{3,2,1,0:T(8,128)(2,1)S(1)}, bf16[6,2,32,512]{3,2,1,0:T(8,128)(2,1)S(1)}, u32[]{:S(2)}, u32[]{:S(2)}) collective-permute-start(bf16[6,2,32,512]{3,2,1,0:T(8,128)(2,1)S(1)} %collective-permute-done.2.refs_3_), channel_id=1, source_target_pairs={{0,84},{1,85},{2,86},{3,87},{4,88},{5,89},{6,90},{7,91},{8,92},{9,... | collective-permute-start | bytes 1179656 | tf_op jit(solution)/shard_map/ppermute | solution.py:28
  82.9 0.0 all-gather.4.cloned.1.call-done
  82.9 0.0 copy-done.3
  82.9 0.0 copy-start
  82.9 2.8 %copy-done = bf16[3072,1024]{1,0:T(8,128)(2,1)S(1)} copy-done((bf16[3072,1024]{1,0:T(8,128)(2,1)S(1)}, bf16[3072,1024]{1,0:T(8,128)(2,1)}, u32[]{:S(2)}) %copy-start) | copy-done | bytes 6291480
  85.7 0.0 copy-start.1
  85.7 2.4 %shard_map.47.refs_8_ = f32[512,1024]{1,0:T(8,128)S(1)} custom-call(s32[1]{0:T(128)} %bitcast.refs_0_, s32[8,48]{1,0:T(8,128)S(1)} %copy-done.3, bf16[6,2,32,512]{3,2,1,0:T(8,128)(2,1)S(1)} %bitcast.14, bf16[6,2,32,512]{3,2,1,0:T(8,128)(2,1)S(1)} %bitcast.11, bf16[2,4,384,1024]{3,2,1,0:T(8,128)(2,1)S(1)} %bitcast.5), custom_call_target="tpu_custom_call" | custom-call | flops 805306368 | bytes 4456448 | tf_op jit(solution)/shard_map/pallas_call | solution.py:104
  88.1 0.0 collective-permute-done.4.refs_2_
  88.1 0.0 collective-permute-done.5.refs_5_
  88.1 0.4 copy-done.1
  88.5 3.9 %shard_map.48.refs_5_ = f32[512,1024]{1,0:T(8,128)S(1)} custom-call(s32[1]{0:T(128)} %bitcast.refs_0_, s32[8,48]{1,0:T(8,128)S(1)} %copy-done.3, bf16[6,2,32,512]{3,2,1,0:T(8,128)(2,1)S(1)} %collective-permute-done.4.refs_2_, bf16[6,2,32,512]{3,2,1,0:T(8,128)(2,1)S(1)} %collective-permute-done.2.refs_3_, ...), custom_call_target="tpu_custom_call" | custom-call | flops 1610612736 | bytes 6815744 | tf_op jit(solution)/shard_map/pallas_call | solution.py:104
  92.4 0.0 collective-permute-done.1.refs_2_
  92.4 0.0 collective-permute-done.3.refs_3_
  92.4 3.4 %shard_map.49 = bf16[512,1024]{1,0:T(8,128)(2,1)} custom-call(s32[1]{0:T(128)} %bitcast.refs_0_, s32[8,48]{1,0:T(8,128)S(1)} %copy-done.3, bf16[6,2,32,512]{3,2,1,0:T(8,128)(2,1)S(1)} %collective-permute-done.1.refs_2_, bf16[6,2,32,512]{3,2,1,0:T(8,128)(2,1)S(1)} %collective-permute-done.3.refs_3_, bf16[2,4,384,1024]{3,2,1,0:T(8,128)(2,1)S(1)} %bitcast.8, ...), custom_call_target="tpu_custom_call" | custom-call | flops 805306368 | bytes 4456448 | tf_op jit(solution)/shard_map/pallas_call | solution.py:104
Async XLA Ops:
  6.5 76.3 %all-gather.4.cloned.1.call-start = ((), (), s32[]{:S(2)}) async-start(), calls=%async_computation.1 | async-start | bytes 7077888 | tf_op jit(solution)/shard_map/all_gather | solution.py:133
  22.2 1.1 %copy-start.2 = (bf16[384,1024]{1,0:T(8,128)(2,1)S(1)}, bf16[384,1024]{1,0:T(8,128)(2,1)}, u32[]{:S(2)}) copy-start(bf16[384,1024]{1,0:T(8,128)(2,1)} %block_ref) | copy-start | bytes 2359300
  23.3 0.7 copy-start.4
  24.0 58.9 %copy-start.3 = (s32[8,48]{1,0:T(8,128)S(1)}, s32[8,48]{1,0:T(8,128)}, u32[]{:S(2)}) copy-start(s32[8,48]{1,0:T(8,128)} %refs_1_.5) | copy-start | bytes 4612
  61.9 13.9 %collective-permute-start = (bf16[6,2,32,512]{3,2,1,0:T(8,128)(2,1)S(1)}, bf16[6,2,32,512]{3,2,1,0:T(8,128)(2,1)S(1)}, u32[]{:S(2)}, u32[]{:S(2)}) collective-permute-start(bf16[6,2,32,512]{3,2,1,0:T(8,128)(2,1)S(1)} %bitcast.12), channel_id=1, source_target_pairs={{0,12},{1,13},{2,14},{3,15},{4,16},{5,17},{6,18},{7,19},{8,20},{9,... | collective-permute-start | bytes 1179656 | tf_op jit(solution)/shard_map/ppermute | solution.py:28
  64.7 13.0 %collective-permute-start.2 = (bf16[6,2,32,512]{3,2,1,0:T(8,128)(2,1)S(1)}, bf16[6,2,32,512]{3,2,1,0:T(8,128)(2,1)S(1)}, u32[]{:S(2)}, u32[]{:S(2)}) collective-permute-start(bf16[6,2,32,512]{3,2,1,0:T(8,128)(2,1)S(1)} %bitcast.9), channel_id=1, source_target_pairs={{0,84},{1,85},{2,86},{3,87},{4,88},{5,89},{6,90},{7,91},{8,92},{9,... | collective-permute-start | bytes 1179656 | tf_op jit(solution)/shard_map/ppermute | solution.py:28
  68.9 19.2 %collective-permute-start.4 = (bf16[6,2,32,512]{3,2,1,0:T(8,128)(2,1)S(1)}, bf16[6,2,32,512]{3,2,1,0:T(8,128)(2,1)S(1)}, u32[]{:S(2)}, u32[]{:S(2)}) collective-permute-start(bf16[6,2,32,512]{3,2,1,0:T(8,128)(2,1)S(1)} %bitcast.13), channel_id=1, source_target_pairs={{0,84},{1,85},{2,86},{3,87},{4,88},{5,89},{6,90},{7,91},{8,92},{9,... | collective-permute-start | bytes 1179656 | tf_op jit(solution)/shard_map/ppermute | solution.py:28
  70.9 17.3 %collective-permute-start.5 = (bf16[6,2,32,512]{3,2,1,0:T(8,128)(2,1)S(1)}, bf16[6,2,32,512]{3,2,1,0:T(8,128)(2,1)S(1)}, u32[]{:S(2)}, u32[]{:S(2)}) collective-permute-start(bf16[6,2,32,512]{3,2,1,0:T(8,128)(2,1)S(1)} %bitcast.10), channel_id=1, source_target_pairs={{0,12},{1,13},{2,14},{3,15},{4,16},{5,17},{6,18},{7,19},{8,20},{9,... | collective-permute-start | bytes 1179656 | tf_op jit(solution)/shard_map/ppermute | solution.py:28
  75.8 16.7 %collective-permute-start.1 = (bf16[6,2,32,512]{3,2,1,0:T(8,128)(2,1)S(1)}, bf16[6,2,32,512]{3,2,1,0:T(8,128)(2,1)S(1)}, u32[]{:S(2)}, u32[]{:S(2)}) collective-permute-start(bf16[6,2,32,512]{3,2,1,0:T(8,128)(2,1)S(1)} %collective-permute-done.refs_4_), channel_id=1, source_target_pairs={{0,12},{1,13},{2,14},{3,15},{4,16},{5,17},{6,18},{7,19},{8,20},{9,... | collective-permute-start | bytes 1179656 | tf_op jit(solution)/shard_map/ppermute | solution.py:28
  77.7 14.7 %collective-permute-start.3 = (bf16[6,2,32,512]{3,2,1,0:T(8,128)(2,1)S(1)}, bf16[6,2,32,512]{3,2,1,0:T(8,128)(2,1)S(1)}, u32[]{:S(2)}, u32[]{:S(2)}) collective-permute-start(bf16[6,2,32,512]{3,2,1,0:T(8,128)(2,1)S(1)} %collective-permute-done.2.refs_3_), channel_id=1, source_target_pairs={{0,84},{1,85},{2,86},{3,87},{4,88},{5,89},{6,90},{7,91},{8,92},{9,... | collective-permute-start | bytes 1179656 | tf_op jit(solution)/shard_map/ppermute | solution.py:28
  82.9 2.8 %copy-start = (bf16[3072,1024]{1,0:T(8,128)(2,1)S(1)}, bf16[3072,1024]{1,0:T(8,128)(2,1)}, u32[]{:S(2)}) copy-start(bf16[3072,1024]{1,0:T(8,128)(2,1)} %all-gather.4.cloned.1.call-done) | copy-start | bytes 18874372
  85.7 2.8 %copy-start.1 = (bf16[3072,1024]{1,0:T(8,128)(2,1)S(1)}, bf16[3072,1024]{1,0:T(8,128)(2,1)}, u32[]{:S(2)}) copy-start(bf16[3072,1024]{1,0:T(8,128)(2,1)} %all-gather.4.cloned.1.call-done) | copy-start | bytes 18874372
Sparse Core Ops, SparseCore 0:
  25.3 50.0 all-gather.3

commit v2 on v0

v2 whole, which is shorter than its diff:
```python
import jax
import jax.numpy as jnp
from jax import lax
from jax.experimental import pallas as pl
from jax.experimental.pallas import tpu as pltpu
from jax.sharding import PartitionSpec as P

TILE = 64
X, CORES, Y, Z = 4, 2, 8, 12
FAR, NEAR = 2, 4
PARTS = 1
VMEM_LIMIT = 20 * 1024 * 1024
HINT = 10**11
SCREEN_VMEM_LIMIT = 60 * 1024 * 1024


def vir(y, z):
    return (y % Y) * Z + z % Z


def occ(x, c):
    return (x % X) * CORES + c


X_GROUPS = [[occ(x, c) for x in range(X)] for c in range(CORES)]
Z_GROUPS = [[vir(y, z) for z in range(Z)] for y in range(Y)]


def shift_y(block, step):
    return lax.ppermute(block, "vir", [(vir(y, z), vir(y + step, z)) for y in range(Y) for z in range(Z)])


def swap_cores(block):
    return lax.ppermute(block, "occ", [(occ(x, c), occ(x, 1 - c)) for x in range(X) for c in range(CORES)])


def after(block, other, flops=0):
    hold = pl.BlockSpec(memory_space=pl.ANY)
    return pl.pallas_call(
        lambda block_ref, other_ref, out_ref: None,
        in_specs=[hold, hold],
        out_specs=hold,
        out_shape=jax.ShapeDtypeStruct(block.shape, block.dtype),
        input_output_aliases={0: 0},
        compiler_params=pltpu.CompilerParams(vmem_limit_bytes=1024 * 1024),
        cost_estimate=pl.CostEstimate(flops=flops, bytes_accessed=0, transcendentals=0),
    )(block, other)


def screen_kernel(mask_ref, block_ref, out_ref, loaded, masked, in_sems, out_sems):
    depth, cols = loaded.shape
    tiles, tile_cols = mask_ref.shape
    copies = out_ref.shape[0]
    part = depth // PARTS
    cuts = [pl.ds(p * part, part) for p in range(PARTS)]
    loads = [pltpu.make_async_copy(block_ref.at[cut, :], loaded.at[cut, :], in_sems.at[p]) for p, cut in enumerate(cuts)]
    for load in loads:
        load.start()
    across = lax.broadcasted_iota(jnp.int32, (tile_cols, cols), 1) // TILE
    spread_to = (across == lax.broadcasted_iota(jnp.int32, (tile_cols, cols), 0)).astype(jnp.float32)
    rows = jnp.dot(mask_ref[...].astype(jnp.float32), spread_to, preferred_element_type=jnp.float32).astype(jnp.bfloat16)
    stores = []
    for p, cut in enumerate(cuts):
        loads[p].wait()
        for t in range(p * tiles // PARTS, (p + 1) * tiles // PARTS):
            at = slice(t * TILE, (t + 1) * TILE)
            masked[at, :] = loaded[at, :] * rows[t : t + 1, :]
        for k in range(copies):
            sem = out_sems.at[p * copies + k]
            stores.append(pltpu.make_async_copy(masked.at[cut, :], out_ref.at[k, cut, :], sem))
            stores[-1].start()
    for store in stores:
        store.wait()


def screen(block, mask, copies):
    hold = pl.BlockSpec(memory_space=pl.ANY)
    return pl.pallas_call(
        screen_kernel,
        in_specs=[pl.BlockSpec(memory_space=pltpu.VMEM), hold],
        out_specs=hold,
        out_shape=jax.ShapeDtypeStruct((copies,) + block.shape, block.dtype),
        scratch_shapes=[
            pltpu.VMEM(block.shape, block.dtype),
            pltpu.VMEM(block.shape, block.dtype),
            pltpu.SemaphoreType.DMA((PARTS,)),
            pltpu.SemaphoreType.DMA((PARTS * copies,)),
        ],
        compiler_params=pltpu.CompilerParams(vmem_limit_bytes=SCREEN_VMEM_LIMIT),
        cost_estimate=pl.CostEstimate(flops=block.size, bytes_accessed=8 * block.size, transcendentals=0),
    )(mask, block)


def product_kernel(origins, has_acc, strips, where, mask_ref, *refs):
    n = len(origins)
    t_refs, refs = refs[: 2 * n], refs[2 * n :]
    own_ref, mate_ref, refs = refs[0], refs[1], refs[2:]
    acc_ref, refs = (refs[0], refs[1:]) if has_acc else (None, refs)
    out_ref, lhs, rhs, row_mask, block, v_sems, out_sems = refs
    some, far, r, rows = t_refs[0].shape
    zs = 2 * some
    cd = zs * r
    per = TILE // r
    wide = out_ref.shape[1] // strips

    def fetch(v_ref, s, q, f):
        y = lax.rem(where[0] + origins[q][0] + NEAR * f, Y)
        k = q * far + f
        source = v_ref.at[y // CORES, :, pl.ds(s * wide, wide)]
        return pltpu.make_async_copy(source, rhs.at[s, pl.ds(k * cd, cd), :], v_sems.at[s * n * far + k])

    for s in range(strips):
        for q in range(n):
            mine = lax.rem(where[0] + origins[q][0], CORES) == where[1]
            for f in range(far):
                pl.when(mine)(lambda: fetch(own_ref, s, q, f).start())
                pl.when(jnp.logical_not(mine))(lambda: fetch(mate_ref, s, q, f).start())

    tiles = mask_ref.shape[1]
    tile_of = lax.broadcasted_iota(jnp.int32, (mask_ref.shape[0], rows), 1) // TILE
    spread_to = (tile_of == lax.broadcasted_iota(jnp.int32, (mask_ref.shape[0], rows), 0)).astype(jnp.float32)
    row_mask[...] = lax.dot_general(
        mask_ref[...].astype(jnp.float32), spread_to, (((0,), (0,)), ((), ())), preferred_element_type=jnp.float32
    )
    for q, halves in enumerate(origins):
        for f in range(far):
            y = lax.rem(where[0] + halves[0] + NEAR * f, Y)
            for z in range(zs):
                half = z // some
                slot = (f + (halves[half] - halves[0]) // NEAR) % far
                mask = row_mask[pl.ds(y * (tiles // Y) + z // per, 1), :].astype(jnp.bfloat16)
                at = (q * far + f) * cd + z * r
                lhs[at : at + r, :] = t_refs[2 * q + half][z % some, slot] * mask

    stores = []
    for s in range(strips):
        for q in range(n):
            for f in range(far):
                fetch(own_ref, s, q, f).wait()
        total = lax.dot_general(lhs[...], rhs[s], (((0,), (0,)), ((), ())), preferred_element_type=jnp.float32)
        if not has_acc:
            out_ref[:, s * wide : (s + 1) * wide] = total
            continue
        block[s] = (total + acc_ref[:, s * wide : (s + 1) * wide]).astype(block.dtype)
        stores.append(pltpu.make_async_copy(block.at[s], out_ref.at[:, pl.ds(s * wide, wide)], out_sems.at[s]))
        stores[-1].start()
    for store in stores:
        store.wait()


def product(where, origins, ts, amp_mask, v_own, v_mate, acc, strips):
    n = len(origins)
    some, far, r, rows = ts[0].shape
    cols = v_own.shape[-1]
    depth = n * 2 * some * far * r
    last = acc is not None
    whole = pl.BlockSpec(memory_space=pltpu.VMEM)
    hold = pl.BlockSpec(memory_space=pl.ANY)
    operands = [where, amp_mask] + list(ts) + [v_own, v_mate] + ([acc] if last else [])
    in_specs = [pl.BlockSpec(memory_space=pltpu.SMEM)] + [whole] * (1 + 2 * n) + [hold] * 2
    dtype = jnp.bfloat16 if last else jnp.float32
    return pl.pallas_call(
        lambda *refs: product_kernel(origins, last, strips, *refs),
        in_specs=in_specs + ([whole] if last else []),
        out_specs=hold if last else whole,
        scratch_shapes=[
            pltpu.VMEM((depth, rows), jnp.bfloat16),
            pltpu.VMEM((strips, depth, cols // strips), jnp.bfloat16),
            pltpu.VMEM((amp_mask.shape[1], rows), jnp.float32),
            pltpu.VMEM((strips, rows, cols // strips) if last else (8, 128), jnp.bfloat16),
            pltpu.SemaphoreType.DMA((strips * n * far,)),
            pltpu.SemaphoreType.DMA((strips,)),
        ],
        out_shape=jax.ShapeDtypeStruct((rows, cols), dtype),
        compiler_params=pltpu.CompilerParams(vmem_limit_bytes=VMEM_LIMIT),
        cost_estimate=pl.CostEstimate(
            flops=2 * rows * cols * depth, bytes_accessed=2 * depth * (rows + cols) + 4 * rows * cols, transcendentals=0
        ),
    )(*operands)


def on_device(amplitudes, integrals, amp_mask, int_mask):
    core = lax.rem(lax.axis_index("occ"), CORES)
    where = jnp.stack([lax.axis_index("vir") // Z, core]).astype(jnp.int32)

    t = amplitudes.T
    other = after(shift_y(t, NEAR), t, flops=HINT)
    v_own = lax.all_to_all(screen(integrals, int_mask, X), "occ", 0, 0, axis_index_groups=X_GROUPS)

    w = lax.all_gather(jnp.stack([t, other]), "vir", axis=0, axis_index_groups=Z_GROUPS)
    v_own = after(v_own, w[0, 0, :16])
    v_mate = swap_cores(v_own)
    w_a, w_b = w[: Z // 2], w[Z // 2 :]
    below_a = shift_y(w_a, 1)
    above_b = shift_y(w_b, -1)
    below_b = shift_y(w_b, 1)
    above_a = after(shift_y(w_a, -1), w[0, 0, :16], flops=HINT)
    two_a = shift_y(below_a, 1)
    two_b = shift_y(above_b, -1)

    ts = (w_a, w_b, above_a, above_b, below_a, below_b)
    acc = product(where, ((0, 0), (1, 1), (Y - 1, Y - 1)), ts, amp_mask, v_own, v_mate, None, 1)
    return product(where, ((Y - 2, 2),), (two_a, two_b), amp_mask, v_own, v_mate, acc, 2)


def solution(mesh):
    return jax.shard_map(
        on_device,
        mesh=mesh,
        in_specs=(P("occ", "vir"), P("occ", "vir"), P("occ", None), P("occ", "vir")),
        out_specs=P("occ", "vir"),
        check_vma=False,
    )
```

time: 207 us -> 93.3 us (0.45)
  waiting for transfers between devices: 179 us -> 5.25 us
  starting transfers between devices: 0.04 us -> 39.5 us
  blocking collectives: 0 us -> 33.2 us
  between operations: 13.4 us -> 0.23 us
  Pallas kernels: 0 us -> 12.2 us
  matrix products: 8.99 us -> 0 us
  other arithmetic: 3.05 us -> 0.6 us
    all_gather x2 -> x0, waiting for transfers between devices: 179 us -> none  [the longest x1 125 us: on_device(): gathered_amps = lax.all_gather(masked_amps, 'vir', axis=1, tiled=True)]
    ppermute x0 -> x8, starting transfers between devices: none -> 35.4 us  [the longest x7 26.5 us: shift_y(): lax.ppermute(block, 'vir', [(vir(y, z), vir(y + step, z)) for y in range(...]
    all_gather x0 -> x1, blocking collectives: none -> 33.2 us  [on_device(): lax.all_gather(jnp.stack([t, other]), 'vir', axis=0, axis_index_groups=Z_...]
    pallas_call x0 -> x6, Pallas kernels: none -> 12.2 us  [the longest x2 8.64 us: product(): pl.pallas_call(lambda *refs: product_kernel(origins, last, strips, *refs)...]
    dot_general x2 -> x0, matrix products: 8.99 us -> none  [the longest x1 8.18 us: on_device(): jnp.dot(gathered_amps, gathered_ints, preferred_element_type=jnp.float32)]
    ppermute x0 -> x8, waiting for transfers between devices: none -> 5.25 us  [the longest x1 5.23 us: swap_cores(): lax.ppermute(block, 'occ', [(occ(x, c), occ(x, 1 - c)) for x in range(X)...]
    all_to_all x0 -> x1, starting transfers between devices: none -> 4.02 us  [on_device(): lax.all_to_all(screen(integrals, int_mask, X), 'occ', 0, 0, axis_index_gr...]
    mul x2 -> x0, other arithmetic: 2.34 us -> none  [the longest x1 1.37 us: on_device(): masked_amps = amplitudes * row_mask]
  transfers between devices with their start and end apart: 2 -> 9, of which waited for: 2 -> 1; matrix products, arithmetic and copies ran while one was open for 2% -> 2% of each run, Pallas kernels for 0% -> 9%
where the time goes in v2:
time: 93.3 us; the launch traced here: 92.6 us
  starting transfers between devices  39.5 us (42%)
  blocking collectives  33.2 us (36%)
  Pallas kernels  12.2 us (13%)
  waiting for transfers between devices  5.25 us (6%)
  local copies, waits for them, and re-layouts  1.66 us (2%)
    all_gather x1, blocking collectives, on_device(): lax.all_gather(jnp.stack([t, other]), 'vir', axis=0, axis_index_groups=Z_...  33.2 us
    ppermute x7, starting transfers between devices, shift_y(): lax.ppermute(block, 'vir', [(vir(y, z), vir(y + step, z)) for y in range(...  26.5 us
    ppermute x1, starting transfers between devices, swap_cores(): lax.ppermute(block, 'occ', [(occ(x, c), occ(x, 1 - c)) for x in range(X)...  8.92 us
    pallas_call x2, Pallas kernels, product(): pl.pallas_call(lambda *refs: product_kernel(origins, last, strips, *refs)...  8.64 us
    ppermute x1, waiting for transfers between devices, swap_cores(): lax.ppermute(block, 'occ', [(occ(x, c), occ(x, 1 - c)) for x in range(X)...  5.23 us
    all_to_all x1, starting transfers between devices, on_device(): lax.all_to_all(screen(integrals, int_mask, X), 'occ', 0, 0, axis_index_gr...  4.02 us
    pallas_call x1, Pallas kernels, screen(): pl.pallas_call(screen_kernel, in_specs=[pl.BlockSpec(memory_space=pltpu.V...  3.55 us
  transfers between devices with their start and end apart: 9, of which 1 were waited for; matrix products, arithmetic and copies ran while one was open for 2% of the time, Pallas kernels for 9%

profile of v2, /device:TPU:1, one launch (start us, length us, event | category | flops | bytes accessed | tf_op | source)
XLA Modules:
  0.0 92.6 jit_solution(3607987565805413441)
XLA Ops:
  0.0 8.3 %collective-permute-start = (bf16[32,512]{1,0:T(8,128)(2,1)}, bf16[32,512]{1,0:T(8,128)(2,1)S(1)}, u32[]{:S(2)}, u32[]{:S(2)}) collective-permute-start(bf16[32,512]{1,0:T(8,128)(2,1)} %bitcast.14), channel_id=1, source_target_pairs={{0,48},{1,49},{2,50},{3,51},{4,52},{5,53},{6,54},{7,55},{8,56},{9,... | collective-permute-start | bytes 98312 | tf_op jit(solution)/shard_map/ppermute | solution.py:30
  8.3 3.5 %shard_map.47 = bf16[4,384,1024]{2,1,0:T(8,128)(2,1)} custom-call(s32[6,16]{1,0:T(8,128)} %mask_ref.1, bf16[384,1024]{1,0:T(8,128)(2,1)} %block_ref.1), custom_call_target="tpu_custom_call" | custom-call | flops 393216 | bytes 3145728 | tf_op jit(solution)/shard_map/pallas_call | solution.py:78
  11.8 0.0 copy-start
  11.9 4.0 %all-to-all-start = ((bf16[4,384,1024]{2,1,0:T(8,128)(2,1)}), bf16[4,384,1024]{2,1,0:T(8,128)(2,1)S(1)}, u32[]{:S(2)}, u32[]{:S(2)}) async-start(bf16[4,384,1024]{2,1,0:T(8,128)(2,1)} %shard_map.47), calls=%async_computation | async-start | bytes 6291456 | tf_op jit(solution)/shard_map/all_to_all | solution.py:188
  15.9 0.0 collective-permute-done.block_ref
  15.9 0.0 copy-done
  15.9 33.2 %all-gather = bf16[24,32,512]{2,1,0:T(8,128)(2,1)S(1)} all-gather(bf16[2,32,512]{2,1,0:T(8,128)(2,1)S(1)} %pad_maximum_fusion), channel_id=2, replica_groups={{0,1,2,3,4,5,6,7,8,9,10,11},{12,13,14,15,16,17,18,19,20,21,22,23},{24,2..., dimensions={0}, use_global_device_ids=true | all-gather | bytes 851968 | tf_op jit(solution)/shard_map/all_gather | solution.py:190
  49.1 0.0 copy-start.3
  49.1 0.9 fusion
  50.0 2.3 %collective-permute-start.1 = (bf16[6,2,32,512]{3,2,1,0:T(8,128)(2,1)}, bf16[6,2,32,512]{3,2,1,0:T(8,128)(2,1)}, u32[]{:S(2)}, u32[]{:S(2)}) collective-permute-start(bf16[6,2,32,512]{3,2,1,0:T(8,128)(2,1)} %bitcast.5.refs_2_), channel_id=1, source_target_pairs={{0,12},{1,13},{2,14},{3,15},{4,16},{5,17},{6,18},{7,19},{8,20},{9,... | collective-permute-start | bytes 1179656 | tf_op jit(solution)/shard_map/ppermute | solution.py:30
  52.3 0.0 copy-done.3
  52.4 4.2 %collective-permute-start.3 = (bf16[6,2,32,512]{3,2,1,0:T(8,128)(2,1)S(1)}, bf16[6,2,32,512]{3,2,1,0:T(8,128)(2,1)}, u32[]{:S(2)}, u32[]{:S(2)}) collective-permute-start(bf16[6,2,32,512]{3,2,1,0:T(8,128)(2,1)S(1)} %bitcast.11), channel_id=1, source_target_pairs={{0,84},{1,85},{2,86},{3,87},{4,88},{5,89},{6,90},{7,91},{8,92},{9,... | collective-permute-start | bytes 1179656 | tf_op jit(solution)/shard_map/ppermute | solution.py:30
  56.6 1.9 %collective-permute-start.6 = (bf16[6,2,32,512]{3,2,1,0:T(8,128)(2,1)}, bf16[6,2,32,512]{3,2,1,0:T(8,128)(2,1)}, u32[]{:S(2)}, u32[]{:S(2)}) collective-permute-start(bf16[6,2,32,512]{3,2,1,0:T(8,128)(2,1)} %bitcast.5.refs_2_), channel_id=1, source_target_pairs={{0,84},{1,85},{2,86},{3,87},{4,88},{5,89},{6,90},{7,91},{8,92},{9,... | collective-permute-start | bytes 1179656 | tf_op jit(solution)/shard_map/ppermute | solution.py:30
  58.5 0.6 pad_add_fusion.refs_0_
  59.1 3.4 %collective-permute-start.7 = (bf16[6,2,32,512]{3,2,1,0:T(8,128)(2,1)S(1)}, bf16[6,2,32,512]{3,2,1,0:T(8,128)(2,1)}, u32[]{:S(2)}, u32[]{:S(2)}) collective-permute-start(bf16[6,2,32,512]{3,2,1,0:T(8,128)(2,1)S(1)} %bitcast.12), channel_id=1, source_target_pairs={{0,12},{1,13},{2,14},{3,15},{4,16},{5,17},{6,18},{7,19},{8,20},{9,... | collective-permute-start | bytes 1179656 | tf_op jit(solution)/shard_map/ppermute | solution.py:30
  62.5 0.7 slice_bitcast_fusion.other_ref
  63.2 0.0 collective-permute-done.1.refs_6_
  63.2 1.9 %collective-permute-start.2 = (bf16[6,2,32,512]{3,2,1,0:T(8,128)(2,1)}, bf16[6,2,32,512]{3,2,1,0:T(8,128)(2,1)}, u32[]{:S(2)}, u32[]{:S(2)}) collective-permute-start(bf16[6,2,32,512]{3,2,1,0:T(8,128)(2,1)} %collective-permute-done.1.refs_6_), channel_id=1, source_target_pairs={{0,12},{1,13},{2,14},{3,15},{4,16},{5,17},{6,18},{7,19},{8,20},{9,... | collective-permute-start | bytes 1179656 | tf_op jit(solution)/shard_map/ppermute | solution.py:30
  65.1 0.0 collective-permute-done.3.refs_5_
  65.1 4.6 %collective-permute-start.4 = (bf16[6,2,32,512]{3,2,1,0:T(8,128)(2,1)}, bf16[6,2,32,512]{3,2,1,0:T(8,128)(2,1)}, u32[]{:S(2)}, u32[]{:S(2)}) collective-permute-start(bf16[6,2,32,512]{3,2,1,0:T(8,128)(2,1)} %collective-permute-done.3.refs_5_), channel_id=1, source_target_pairs={{0,84},{1,85},{2,86},{3,87},{4,88},{5,89},{6,90},{7,91},{8,92},{9,... | collective-permute-start | bytes 1179656 | tf_op jit(solution)/shard_map/ppermute | solution.py:30
  69.7 0.0 all-to-all-done.block_ref
  69.7 0.0 copy-start.1
  69.7 0.0 copy-start.2
  69.7 8.9 %collective-permute-start.5 = (bf16[4,384,1024]{2,1,0:T(8,128)(2,1)S(1)}, bf16[4,384,1024]{2,1,0:T(8,128)(2,1)S(1)}, u32[]{:S(2)}, u32[]{:S(2)}) collective-permute-start(bf16[4,384,1024]{2,1,0:T(8,128)(2,1)S(1)} %shard_map.48.refs_8_.refs_4_), channel_id=1, source_target_pairs={{0,96},{96,0},{192,288},{288,192},{384,480},{480,384},{576,672},{6... | collective-permute-start | bytes 9437192 | tf_op jit(solution)/shard_map/ppermute | solution.py:34
  78.7 0.0 collective-permute-done.6.block_ref
  78.7 0.0 collective-permute-done.7.refs_7_
  78.7 5.2 %collective-permute-done.5.refs_9_.refs_5_ = bf16[4,384,1024]{2,1,0:T(8,128)(2,1)S(1)} collective-permute-done((bf16[4,384,1024]{2,1,0:T(8,128)(2,1)S(1)}, bf16[4,384,1024]{2,1,0:T(8,128)(2,1)S(1)}, u32[]{:S(2)}, u32[]{:S(2)}) %collective-permute-start.5) | collective-permute-done | bytes 3145760 | tf_op jit(solution)/shard_map/ppermute | solution.py:34
  83.9 0.0 copy-done.1
  83.9 0.0 copy-done.2
  83.9 5.0 %shard_map.50.refs_6_ = f32[512,1024]{1,0:T(8,128)S(1)} custom-call(s32[2]{0:T(128)S(1)} %copy-done.2, s32[8,48]{1,0:T(8,128)S(1)} %copy-done.1, bf16[6,2,32,512]{3,2,1,0:T(8,128)(2,1)} %bitcast.5.refs_2_, bf16[6,2,32,512]{3,2,1,0:T(8,128)(2,1)S(1)} %bitcast.13, bf16[6,2,32,512]{3,2,1,0:T(8,128)(2,1)} %shard_map.49.refs_4_, ...), custom_call_target="tpu_custom_call" | custom-call | flops 2415919104 | bytes 9175040 | tf_op jit(solution)/shard_map/pallas_call | solution.py:162
  89.0 0.0 collective-permute-done.2.refs_2_
  89.0 0.0 collective-permute-done.4.refs_3_
  89.0 3.6 %shard_map.51 = bf16[512,1024]{1,0:T(8,128)(2,1)} custom-call(s32[2]{0:T(128)S(1)} %copy-done.2, s32[8,48]{1,0:T(8,128)S(1)} %copy-done.1, bf16[6,2,32,512]{3,2,1,0:T(8,128)(2,1)} %collective-permute-done.2.refs_2_, bf16[6,2,32,512]{3,2,1,0:T(8,128)(2,1)} %collective-permute-done.4.refs_3_, bf16[4,384,1024]{2,1,0:T(8,128)(2,1)S(1)} %shard_map.48.refs_8_.refs_4_, ...), custom_call_target="tpu_custom_call" | custom-call | flops 805306368 | bytes 4456448 | tf_op jit(solution)/shard_map/pallas_call | solution.py:162
  (4 shorter events, 0.0 us)
Async XLA Ops:
  0.0 15.9 %collective-permute-start = (bf16[32,512]{1,0:T(8,128)(2,1)}, bf16[32,512]{1,0:T(8,128)(2,1)S(1)}, u32[]{:S(2)}, u32[]{:S(2)}) collective-permute-start(bf16[32,512]{1,0:T(8,128)(2,1)} %bitcast.14), channel_id=1, source_target_pairs={{0,48},{1,49},{2,50},{3,51},{4,52},{5,53},{6,54},{7,55},{8,56},{9,... | collective-permute-start | bytes 98312 | tf_op jit(solution)/shard_map/ppermute | solution.py:30
  11.8 4.0 %copy-start = (bf16[512,32]{0,1:T(8,128)(2,1)S(1)}, bf16[512,32]{0,1:T(8,128)(2,1)}, u32[]{:S(2)}) copy-start(bf16[512,32]{0,1:T(8,128)(2,1)} %param.4) | copy-start | bytes 98308
  11.9 57.8 %all-to-all-start = ((bf16[4,384,1024]{2,1,0:T(8,128)(2,1)}), bf16[4,384,1024]{2,1,0:T(8,128)(2,1)S(1)}, u32[]{:S(2)}, u32[]{:S(2)}) async-start(bf16[4,384,1024]{2,1,0:T(8,128)(2,1)} %shard_map.47), calls=%async_computation | async-start | bytes 6291456 | tf_op jit(solution)/shard_map/all_to_all | solution.py:188
  49.1 3.2 %copy-start.3 = (bf16[24,32,512]{2,1,0:T(8,128)(2,1)}, bf16[24,32,512]{2,1,0:T(8,128)(2,1)S(1)}, u32[]{:S(2)}) copy-start(bf16[24,32,512]{2,1,0:T(8,128)(2,1)S(1)} %all-gather) | copy-start | bytes 2359300
  50.0 13.1 %collective-permute-start.1 = (bf16[6,2,32,512]{3,2,1,0:T(8,128)(2,1)}, bf16[6,2,32,512]{3,2,1,0:T(8,128)(2,1)}, u32[]{:S(2)}, u32[]{:S(2)}) collective-permute-start(bf16[6,2,32,512]{3,2,1,0:T(8,128)(2,1)} %bitcast.5.refs_2_), channel_id=1, source_target_pairs={{0,12},{1,13},{2,14},{3,15},{4,16},{5,17},{6,18},{7,19},{8,20},{9,... | collective-permute-start | bytes 1179656 | tf_op jit(solution)/shard_map/ppermute | solution.py:30
  52.4 12.8 %collective-permute-start.3 = (bf16[6,2,32,512]{3,2,1,0:T(8,128)(2,1)S(1)}, bf16[6,2,32,512]{3,2,1,0:T(8,128)(2,1)}, u32[]{:S(2)}, u32[]{:S(2)}) collective-permute-start(bf16[6,2,32,512]{3,2,1,0:T(8,128)(2,1)S(1)} %bitcast.11), channel_id=1, source_target_pairs={{0,84},{1,85},{2,86},{3,87},{4,88},{5,89},{6,90},{7,91},{8,92},{9,... | collective-permute-start | bytes 1179656 | tf_op jit(solution)/shard_map/ppermute | solution.py:30
  56.6 22.1 %collective-permute-start.6 = (bf16[6,2,32,512]{3,2,1,0:T(8,128)(2,1)}, bf16[6,2,32,512]{3,2,1,0:T(8,128)(2,1)}, u32[]{:S(2)}, u32[]{:S(2)}) collective-permute-start(bf16[6,2,32,512]{3,2,1,0:T(8,128)(2,1)} %bitcast.5.refs_2_), channel_id=1, source_target_pairs={{0,84},{1,85},{2,86},{3,87},{4,88},{5,89},{6,90},{7,91},{8,92},{9,... | collective-permute-start | bytes 1179656 | tf_op jit(solution)/shard_map/ppermute | solution.py:30
  59.1 19.6 %collective-permute-start.7 = (bf16[6,2,32,512]{3,2,1,0:T(8,128)(2,1)S(1)}, bf16[6,2,32,512]{3,2,1,0:T(8,128)(2,1)}, u32[]{:S(2)}, u32[]{:S(2)}) collective-permute-start(bf16[6,2,32,512]{3,2,1,0:T(8,128)(2,1)S(1)} %bitcast.12), channel_id=1, source_target_pairs={{0,12},{1,13},{2,14},{3,15},{4,16},{5,17},{6,18},{7,19},{8,20},{9,... | collective-permute-start | bytes 1179656 | tf_op jit(solution)/shard_map/ppermute | solution.py:30
  63.2 25.8 %collective-permute-start.2 = (bf16[6,2,32,512]{3,2,1,0:T(8,128)(2,1)}, bf16[6,2,32,512]{3,2,1,0:T(8,128)(2,1)}, u32[]{:S(2)}, u32[]{:S(2)}) collective-permute-start(bf16[6,2,32,512]{3,2,1,0:T(8,128)(2,1)} %collective-permute-done.1.refs_6_), channel_id=1, source_target_pairs={{0,12},{1,13},{2,14},{3,15},{4,16},{5,17},{6,18},{7,19},{8,20},{9,... | collective-permute-start | bytes 1179656 | tf_op jit(solution)/shard_map/ppermute | solution.py:30
  65.1 23.9 %collective-permute-start.4 = (bf16[6,2,32,512]{3,2,1,0:T(8,128)(2,1)}, bf16[6,2,32,512]{3,2,1,0:T(8,128)(2,1)}, u32[]{:S(2)}, u32[]{:S(2)}) collective-permute-start(bf16[6,2,32,512]{3,2,1,0:T(8,128)(2,1)} %collective-permute-done.3.refs_5_), channel_id=1, source_target_pairs={{0,84},{1,85},{2,86},{3,87},{4,88},{5,89},{6,90},{7,91},{8,92},{9,... | collective-permute-start | bytes 1179656 | tf_op jit(solution)/shard_map/ppermute | solution.py:30
  69.7 14.2 %copy-start.1 = (s32[8,48]{1,0:T(8,128)S(1)}, s32[8,48]{1,0:T(8,128)}, u32[]{:S(2)}) copy-start(s32[8,48]{1,0:T(8,128)} %refs_1_.3) | copy-start | bytes 4612
  69.7 14.2 %copy-start.2 = (s32[2]{0:T(128)S(1)}, s32[2]{0:T(128)}, u32[]{:S(2)}) copy-start(s32[2]{0:T(128)} %pad_add_fusion.refs_0_) | copy-start | bytes 28
  69.7 14.2 %collective-permute-start.5 = (bf16[4,384,1024]{2,1,0:T(8,128)(2,1)S(1)}, bf16[4,384,1024]{2,1,0:T(8,128)(2,1)S(1)}, u32[]{:S(2)}, u32[]{:S(2)}) collective-permute-start(bf16[4,384,1024]{2,1,0:T(8,128)(2,1)S(1)} %shard_map.48.refs_8_.refs_4_), channel_id=1, source_target_pairs={{0,96},{96,0},{192,288},{288,192},{384,480},{480,384},{576,672},{6... | collective-permute-start | bytes 9437192 | tf_op jit(solution)/shard_map/ppermute | solution.py:34

commit v3 on v0

v3 whole, which is shorter than its diff:
```python
import jax
import jax.numpy as jnp
from jax import lax
from jax.experimental import pallas as pl
from jax.experimental.pallas import tpu as pltpu
from jax.sharding import PartitionSpec as P

TILE = 64
X, CORES, Y, Z = 4, 2, 8, 12
FAR, NEAR = 2, 4
STRIPS = 2
VMEM_LIMIT = 20 * 1024 * 1024
HINT = 10**11
SCREEN_VMEM_LIMIT = 60 * 1024 * 1024


def vir(y, z):
    return (y % Y) * Z + z % Z


def occ(x, c):
    return (x % X) * CORES + c


X_GROUPS = [[occ(x, c) for x in range(X)] for c in range(CORES)]
Z_GROUPS = [[vir(y, z) for z in range(Z)] for y in range(Y)]


def shift_y(block, step):
    return lax.ppermute(block, "vir", [(vir(y, z), vir(y + step, z)) for y in range(Y) for z in range(Z)])


def swap_cores(block):
    return lax.ppermute(block, "occ", [(occ(x, c), occ(x, 1 - c)) for x in range(X) for c in range(CORES)])


def after(block, other, flops=0):
    hold = pl.BlockSpec(memory_space=pl.ANY)
    return pl.pallas_call(
        lambda block_ref, other_ref, out_ref: None,
        in_specs=[hold, hold],
        out_specs=hold,
        out_shape=jax.ShapeDtypeStruct(block.shape, block.dtype),
        input_output_aliases={0: 0},
        compiler_params=pltpu.CompilerParams(vmem_limit_bytes=1024 * 1024),
        cost_estimate=pl.CostEstimate(flops=flops, bytes_accessed=0, transcendentals=0),
    )(block, other)


def screen_kernel(mask_ref, block_ref, out_ref, masked, sems):
    depth, cols = block_ref.shape
    tiles, tile_cols = mask_ref.shape
    across = lax.broadcasted_iota(jnp.int32, (tile_cols, cols), 1) // TILE
    spread_to = (across == lax.broadcasted_iota(jnp.int32, (tile_cols, cols), 0)).astype(jnp.float32)
    rows = jnp.dot(mask_ref[...].astype(jnp.float32), spread_to, preferred_element_type=jnp.float32).astype(jnp.bfloat16)
    for t in range(tiles):
        part = slice(t * TILE, (t + 1) * TILE)
        masked[part, :] = block_ref[part, :] * rows[t : t + 1, :]
    copies = [pltpu.make_async_copy(masked, out_ref.at[k], sems.at[k]) for k in range(out_ref.shape[0])]
    for copy in copies:
        copy.start()
    for copy in copies:
        copy.wait()


def screen(block, mask, copies):
    whole = pl.BlockSpec(memory_space=pltpu.VMEM)
    return pl.pallas_call(
        screen_kernel,
        in_specs=[whole, whole],
        out_specs=pl.BlockSpec(memory_space=pl.ANY),
        out_shape=jax.ShapeDtypeStruct((copies,) + block.shape, block.dtype),
        scratch_shapes=[pltpu.VMEM(block.shape, block.dtype), pltpu.SemaphoreType.DMA((copies,))],
        compiler_params=pltpu.CompilerParams(vmem_limit_bytes=SCREEN_VMEM_LIMIT),
        cost_estimate=pl.CostEstimate(flops=block.size, bytes_accessed=8 * block.size, transcendentals=0),
    )(mask, block)


def spread_mask(mask_ref, row_mask):
    tile_of = lax.broadcasted_iota(jnp.int32, (mask_ref.shape[0], row_mask.shape[1]), 1) // TILE
    spread_to = (tile_of == lax.broadcasted_iota(jnp.int32, tile_of.shape, 0)).astype(jnp.float32)
    row_mask[...] = lax.dot_general(
        mask_ref[...].astype(jnp.float32), spread_to, (((0,), (0,)), ((), ())), preferred_element_type=jnp.float32
    )


def load_t(t_refs, loaded, sems):
    copies = [pltpu.make_async_copy(t, loaded.at[i], sems.at[i]) for i, t in enumerate(t_refs)]
    for copy in copies:
        copy.start()
    return copies


def screen_t(halves, q, copies, loaded, row_mask, lhs):
    some, far, r = loaded.shape[1:4]
    cd = 2 * some * r
    tiles = row_mask.shape[0]
    here = lax.axis_index("vir") // Z
    for half in range(2):
        copies[2 * q + half].wait()
        for f in range(far):
            y = lax.rem(here + halves[0] + NEAR * f, Y)
            slot = (f + (halves[half] - halves[0]) // NEAR) % FAR
            for z in range(some):
                tile = y * (tiles // Y) + (half * some + z) // (TILE // r)
                mask = row_mask[pl.ds(tile, 1), :].astype(jnp.bfloat16)
                at = (q * far + f) * cd + (half * some + z) * r
                lhs[at : at + r, :] = loaded[2 * q + half, z, slot] * mask


def fetch_v(offset, own_ref, mate_ref, target, sem, go):
    y = lax.rem(lax.axis_index("vir") // Z + offset, Y)
    mine = lax.rem(y, CORES) == lax.rem(lax.axis_index("occ"), CORES)
    if go:
        pl.when(mine)(lambda: pltpu.make_async_copy(own_ref.at[y // CORES], target, sem).start())
        pl.when(jnp.logical_not(mine))(lambda: pltpu.make_async_copy(mate_ref.at[y // CORES], target, sem).start())
    else:
        pltpu.make_async_copy(own_ref.at[y // CORES], target, sem).wait()


def first_kernel(origins, after_these, mask_ref, *refs):
    n = len(origins)
    t_refs, refs = refs[: 2 * n], refs[2 * n :]
    own_ref, mate_ref, out_ref, later_ref, loaded, lhs, rhs, row_mask, t_sems, v_sems = refs
    cd = own_ref.shape[1]

    def fetches(go):
        for i, halves in enumerate(origins):
            for f in range(FAR):
                k = i * FAR + f
                fetch_v(halves[0] + NEAR * f, own_ref, mate_ref, rhs.at[pl.ds(k * cd, cd), :], v_sems.at[k], go)

    def later(go):
        for f in range(FAR):
            sem = v_sems.at[n * FAR + f]
            fetch_v(after_these + NEAR * f, own_ref, mate_ref, later_ref.at[pl.ds(f * cd, cd), :], sem, go)

    copies = load_t(t_refs, loaded, t_sems)
    fetches(True)
    later(True)
    spread_mask(mask_ref, row_mask)
    for q, halves in enumerate(origins):
        screen_t(halves, q, copies, loaded, row_mask, lhs)
    fetches(False)
    out_ref[...] = lax.dot_general(lhs[...], rhs[...], (((0,), (0,)), ((), ())), preferred_element_type=jnp.float32)
    later(False)


def last_kernel(halves, mask_ref, a_ref, b_ref, v_ref, acc_ref, out_ref, loaded, lhs, row_mask, block, t_sems, out_sems):
    copies = load_t((a_ref, b_ref), loaded, t_sems)
    spread_mask(mask_ref, row_mask)
    screen_t(halves, 0, copies, loaded, row_mask, lhs)
    strips = block.shape[0]
    wide = block.shape[2]
    stores = []
    for s in range(strips):
        columns = slice(s * wide, (s + 1) * wide)
        total = lax.dot_general(lhs[...], v_ref[:, columns], (((0,), (0,)), ((), ())), preferred_element_type=jnp.float32)
        block[s] = (total + acc_ref[:, columns]).astype(block.dtype)
        stores.append(pltpu.make_async_copy(block.at[s], out_ref.at[:, pl.ds(s * wide, wide)], out_sems.at[s]))
        stores[-1].start()
    for store in stores:
        store.wait()


WHOLE = pl.BlockSpec(memory_space=pltpu.VMEM)
HOLD = pl.BlockSpec(memory_space=pl.ANY)


def hint(rows, cols, depth):
    return pl.CostEstimate(
        flops=2 * rows * cols * depth, bytes_accessed=2 * depth * (rows + cols) + 4 * rows * cols, transcendentals=0
    )


def first_product(origins, after_these, ts, amp_mask, v_own, v_mate):
    n = len(origins)
    rows = ts[0].shape[-1]
    cd, cols = v_own.shape[1:]
    depth = n * FAR * cd
    return pl.pallas_call(
        lambda *refs: first_kernel(origins, after_these, *refs),
        in_specs=[WHOLE] + [HOLD] * (2 * n + 2),
        out_specs=(WHOLE, WHOLE),
        out_shape=(jax.ShapeDtypeStruct((rows, cols), jnp.float32), jax.ShapeDtypeStruct((FAR * cd, cols), v_own.dtype)),
        scratch_shapes=[
            pltpu.VMEM((2 * n,) + ts[0].shape, jnp.bfloat16),
            pltpu.VMEM((depth, rows), jnp.bfloat16),
            pltpu.VMEM((depth, cols), jnp.bfloat16),
            pltpu.VMEM((amp_mask.shape[1], rows), jnp.float32),
            pltpu.SemaphoreType.DMA((2 * n,)),
            pltpu.SemaphoreType.DMA(((n + 1) * FAR,)),
        ],
        compiler_params=pltpu.CompilerParams(vmem_limit_bytes=VMEM_LIMIT),
        cost_estimate=hint(rows, cols, depth),
    )(amp_mask, *ts, v_own, v_mate)


def last_product(halves, t_a, t_b, amp_mask, v, acc):
    rows, cols = acc.shape
    depth = v.shape[0]
    return pl.pallas_call(
        lambda *refs: last_kernel(halves, *refs),
        in_specs=[WHOLE, HOLD, HOLD, WHOLE, WHOLE],
        out_specs=HOLD,
        out_shape=jax.ShapeDtypeStruct((rows, cols), jnp.bfloat16),
        scratch_shapes=[
            pltpu.VMEM((2,) + t_a.shape, jnp.bfloat16),
            pltpu.VMEM((depth, rows), jnp.bfloat16),
            pltpu.VMEM((amp_mask.shape[1], rows), jnp.float32),
            pltpu.VMEM((STRIPS, rows, cols // STRIPS), jnp.bfloat16),
            pltpu.SemaphoreType.DMA((2,)),
            pltpu.SemaphoreType.DMA((STRIPS,)),
        ],
        compiler_params=pltpu.CompilerParams(vmem_limit_bytes=VMEM_LIMIT),
        cost_estimate=hint(rows, cols, depth),
    )(amp_mask, t_a, t_b, v, acc)


def on_device(amplitudes, integrals, amp_mask, int_mask):
    t = amplitudes.T
    other = after(shift_y(t, NEAR), t, flops=HINT)
    v_own = lax.all_to_all(screen(integrals, int_mask, X), "occ", 0, 0, axis_index_groups=X_GROUPS)

    w = lax.all_gather(jnp.stack([t, other]), "vir", axis=0, axis_index_groups=Z_GROUPS)
    w_a, w_b = w[: Z // 2], w[Z // 2 :]
    v_own = after(v_own, w_b)
    v_mate = swap_cores(v_own)
    below_a = shift_y(w_a, 1)
    above_b = shift_y(w_b, -1)
    below_b = shift_y(w_b, 1)
    above_a = after(shift_y(w_a, -1), w_b, flops=HINT)
    two_a = shift_y(below_a, 1)
    two_b = shift_y(above_b, -1)

    ts = (w_a, w_b, above_a, above_b, below_a, below_b)
    acc, v_two = first_product(((0, 0), (1, 1), (Y - 1, Y - 1)), Y - 2, ts, amp_mask, v_own, v_mate)
    return last_product((Y - 2, 2), two_a, two_b, amp_mask, v_two, acc)


def solution(mesh):
    return jax.shard_map(
        on_device,
        mesh=mesh,
        in_specs=(P("occ", "vir"), P("occ", "vir"), P("occ", None), P("occ", "vir")),
        out_specs=P("occ", "vir"),
        check_vma=False,
    )
```

time: 207 us -> 89.9 us (0.43)
  waiting for transfers between devices: 179 us -> 5.25 us
  starting transfers between devices: 0.04 us -> 39.5 us
  blocking collectives: 0 us -> 33.2 us
  between operations: 13.4 us -> 0.19 us
  Pallas kernels: 0 us -> 10.4 us
  matrix products: 8.99 us -> 0 us
  other arithmetic: 3.05 us -> 0.01 us
    all_gather x2 -> x0, waiting for transfers between devices: 179 us -> none  [the longest x1 125 us: on_device(): gathered_amps = lax.all_gather(masked_amps, 'vir', axis=1, tiled=True)]
    ppermute x0 -> x8, starting transfers between devices: none -> 35.5 us  [the longest x7 25.3 us: shift_y(): lax.ppermute(block, 'vir', [(vir(y, z), vir(y + step, z)) for y in range(...]
    all_gather x0 -> x1, blocking collectives: none -> 33.2 us  [on_device(): lax.all_gather(jnp.stack([t, other]), 'vir', axis=0, axis_index_groups=Z_...]
    pallas_call x0 -> x6, Pallas kernels: none -> 10.4 us  [the longest x1 4.36 us: first_product(): pl.pallas_call(lambda *refs: first_kernel(origins, after_these, *refs), i...]
    dot_general x2 -> x0, matrix products: 8.99 us -> none  [the longest x1 8.18 us: on_device(): jnp.dot(gathered_amps, gathered_ints, preferred_element_type=jnp.float32)]
    ppermute x0 -> x8, waiting for transfers between devices: none -> 5.25 us  [the longest x1 5.23 us: swap_cores(): lax.ppermute(block, 'occ', [(occ(x, c), occ(x, 1 - c)) for x in range(X)...]
    all_to_all x0 -> x1, starting transfers between devices: none -> 4.02 us  [on_device(): lax.all_to_all(screen(integrals, int_mask, X), 'occ', 0, 0, axis_index_gr...]
    mul x2 -> x0, other arithmetic: 2.34 us -> none  [the longest x1 1.37 us: on_device(): masked_amps = amplitudes * row_mask]
  transfers between devices with their start and end apart: 2 -> 9, of which waited for: 2 -> 1; matrix products, arithmetic and copies ran while one was open for 2% -> 1% of each run, Pallas kernels for 0% -> 8%
where the time goes in v3:
time: 89.9 us; the launch traced here: 89.4 us
  starting transfers between devices  39.5 us (44%)
  blocking collectives  33.2 us (37%)
  Pallas kernels  10.4 us (12%)
  waiting for transfers between devices  5.25 us (6%)
    all_gather x1, blocking collectives, on_device(): lax.all_gather(jnp.stack([t, other]), 'vir', axis=0, axis_index_groups=Z_...  33.2 us
    ppermute x7, starting transfers between devices, shift_y(): lax.ppermute(block, 'vir', [(vir(y, z), vir(y + step, z)) for y in range(...  25.3 us
    ppermute x1, starting transfers between devices, swap_cores(): lax.ppermute(block, 'occ', [(occ(x, c), occ(x, 1 - c)) for x in range(X)...  10.2 us
    ppermute x1, waiting for transfers between devices, swap_cores(): lax.ppermute(block, 'occ', [(occ(x, c), occ(x, 1 - c)) for x in range(X)...  5.23 us
    pallas_call x1, Pallas kernels, first_product(): pl.pallas_call(lambda *refs: first_kernel(origins, after_these, *refs), i...  4.36 us
    all_to_all x1, starting transfers between devices, on_device(): lax.all_to_all(screen(integrals, int_mask, X), 'occ', 0, 0, axis_index_gr...  4.02 us
    pallas_call x1, Pallas kernels, screen(): pl.pallas_call(screen_kernel, in_specs=[whole, whole], out_specs=pl.Block...  3.03 us
    pallas_call x1, Pallas kernels, last_product(): pl.pallas_call(lambda *refs: last_kernel(halves, *refs), in_specs=[WHOLE,...  2.98 us
  transfers between devices with their start and end apart: 9, of which 1 were waited for; matrix products, arithmetic and copies ran while one was open for 1% of the time, Pallas kernels for 8%

profile of v3, /device:TPU:1, one launch (start us, length us, event | category | flops | bytes accessed | tf_op | source)
XLA Modules:
  0.0 89.4 jit_solution(14151155621513251266)
XLA Ops:
  0.0 8.3 %collective-permute-start = (bf16[32,512]{1,0:T(8,128)(2,1)}, bf16[32,512]{1,0:T(8,128)(2,1)S(1)}, u32[]{:S(2)}, u32[]{:S(2)}) collective-permute-start(bf16[32,512]{1,0:T(8,128)(2,1)} %bitcast.11), channel_id=1, source_target_pairs={{0,48},{1,49},{2,50},{3,51},{4,52},{5,53},{6,54},{7,55},{8,56},{9,... | collective-permute-start | bytes 98312 | tf_op jit(solution)/shard_map/ppermute | solution.py:30
  8.3 3.0 %shard_map.48 = bf16[4,384,1024]{2,1,0:T(8,128)(2,1)} custom-call(s32[6,16]{1,0:T(8,128)} %mask_ref.1, bf16[384,1024]{1,0:T(8,128)(2,1)} %block_ref.1), custom_call_target="tpu_custom_call" | custom-call | flops 393216 | bytes 3145728 | tf_op jit(solution)/shard_map/pallas_call | solution.py:68
  11.3 0.0 copy-start
  11.3 4.0 %all-to-all-start = ((bf16[4,384,1024]{2,1,0:T(8,128)(2,1)}), bf16[4,384,1024]{2,1,0:T(8,128)(2,1)S(1)}, u32[]{:S(2)}, u32[]{:S(2)}) async-start(bf16[4,384,1024]{2,1,0:T(8,128)(2,1)} %shard_map.48), calls=%async_computation | async-start | bytes 6291456 | tf_op jit(solution)/shard_map/all_to_all | solution.py:223
  15.4 0.0 collective-permute-done.block_ref
  15.4 0.0 copy-done
  15.4 33.2 %all-gather = bf16[24,32,512]{2,1,0:T(8,128)(2,1)S(1)} all-gather(bf16[2,32,512]{2,1,0:T(8,128)(2,1)S(1)} %pad_maximum_fusion), channel_id=2, replica_groups={{0,1,2,3,4,5,6,7,8,9,10,11},{12,13,14,15,16,17,18,19,20,21,22,23},{24,2..., dimensions={0}, use_global_device_ids=true | all-gather | bytes 851968 | tf_op jit(solution)/shard_map/all_gather | solution.py:225
  48.6 0.8 fusion
  49.4 2.1 %collective-permute-start.3 = (bf16[6,2,32,512]{3,2,1,0:T(8,128)(2,1)S(1)}, bf16[6,2,32,512]{3,2,1,0:T(8,128)(2,1)}, u32[]{:S(2)}, u32[]{:S(2)}) collective-permute-start(bf16[6,2,32,512]{3,2,1,0:T(8,128)(2,1)S(1)} %bitcast.6), channel_id=1, source_target_pairs={{0,84},{1,85},{2,86},{3,87},{4,88},{5,89},{6,90},{7,91},{8,92},{9,... | collective-permute-start | bytes 1179656 | tf_op jit(solution)/shard_map/ppermute | solution.py:30
  51.5 3.2 %collective-permute-start.1 = (bf16[6,2,32,512]{3,2,1,0:T(8,128)(2,1)}, bf16[6,2,32,512]{3,2,1,0:T(8,128)(2,1)}, u32[]{:S(2)}, u32[]{:S(2)}) collective-permute-start(bf16[6,2,32,512]{3,2,1,0:T(8,128)(2,1)} %bitcast.3.refs_1_), channel_id=1, source_target_pairs={{0,12},{1,13},{2,14},{3,15},{4,16},{5,17},{6,18},{7,19},{8,20},{9,... | collective-permute-start | bytes 1179656 | tf_op jit(solution)/shard_map/ppermute | solution.py:30
  54.7 3.3 %collective-permute-start.5 = (bf16[6,2,32,512]{3,2,1,0:T(8,128)(2,1)}, bf16[6,2,32,512]{3,2,1,0:T(8,128)(2,1)}, u32[]{:S(2)}, u32[]{:S(2)}) collective-permute-start(bf16[6,2,32,512]{3,2,1,0:T(8,128)(2,1)} %bitcast.3.refs_1_), channel_id=1, source_target_pairs={{0,84},{1,85},{2,86},{3,87},{4,88},{5,89},{6,90},{7,91},{8,92},{9,... | collective-permute-start | bytes 1179656 | tf_op jit(solution)/shard_map/ppermute | solution.py:30
  58.0 2.0 %collective-permute-start.6 = (bf16[6,2,32,512]{3,2,1,0:T(8,128)(2,1)S(1)}, bf16[6,2,32,512]{3,2,1,0:T(8,128)(2,1)}, u32[]{:S(2)}, u32[]{:S(2)}) collective-permute-start(bf16[6,2,32,512]{3,2,1,0:T(8,128)(2,1)S(1)} %bitcast.7), channel_id=1, source_target_pairs={{0,12},{1,13},{2,14},{3,15},{4,16},{5,17},{6,18},{7,19},{8,20},{9,... | collective-permute-start | bytes 1179656 | tf_op jit(solution)/shard_map/ppermute | solution.py:30
  60.0 0.0 collective-permute-done.3.refs_4_
  60.0 4.5 %collective-permute-start.4 = (bf16[6,2,32,512]{3,2,1,0:T(8,128)(2,1)}, bf16[6,2,32,512]{3,2,1,0:T(8,128)(2,1)}, u32[]{:S(2)}, u32[]{:S(2)}) collective-permute-start(bf16[6,2,32,512]{3,2,1,0:T(8,128)(2,1)} %collective-permute-done.3.refs_4_), channel_id=1, source_target_pairs={{0,84},{1,85},{2,86},{3,87},{4,88},{5,89},{6,90},{7,91},{8,92},{9,... | collective-permute-start | bytes 1179656 | tf_op jit(solution)/shard_map/ppermute | solution.py:30
  64.5 0.0 collective-permute-done.1.refs_5_
  64.5 1.9 %collective-permute-start.2 = (bf16[6,2,32,512]{3,2,1,0:T(8,128)(2,1)}, bf16[6,2,32,512]{3,2,1,0:T(8,128)(2,1)}, u32[]{:S(2)}, u32[]{:S(2)}) collective-permute-start(bf16[6,2,32,512]{3,2,1,0:T(8,128)(2,1)} %collective-permute-done.1.refs_5_), channel_id=1, source_target_pairs={{0,12},{1,13},{2,14},{3,15},{4,16},{5,17},{6,18},{7,19},{8,20},{9,... | collective-permute-start | bytes 1179656 | tf_op jit(solution)/shard_map/ppermute | solution.py:30
  66.5 0.0 all-to-all-done.block_ref
  66.5 0.0 copy-start.1
  66.5 10.2 %collective-permute-start.7 = (bf16[4,384,1024]{2,1,0:T(8,128)(2,1)S(1)}, bf16[4,384,1024]{2,1,0:T(8,128)(2,1)S(1)}, u32[]{:S(2)}, u32[]{:S(2)}) collective-permute-start(bf16[4,384,1024]{2,1,0:T(8,128)(2,1)S(1)} %shard_map.49.refs_7_), channel_id=1, source_target_pairs={{0,96},{96,0},{192,288},{288,192},{384,480},{480,384},{576,672},{6... | collective-permute-start | bytes 9437192 | tf_op jit(solution)/shard_map/ppermute | solution.py:34
  76.7 0.0 collective-permute-done.5.block_ref
  76.7 0.0 collective-permute-done.6.refs_6_
  76.8 5.2 %collective-permute-done.7.refs_8_ = bf16[4,384,1024]{2,1,0:T(8,128)(2,1)S(1)} collective-permute-done((bf16[4,384,1024]{2,1,0:T(8,128)(2,1)S(1)}, bf16[4,384,1024]{2,1,0:T(8,128)(2,1)S(1)}, u32[]{:S(2)}, u32[]{:S(2)}) %collective-permute-start.7) | collective-permute-done | bytes 3145760 | tf_op jit(solution)/shard_map/ppermute | solution.py:34
  82.0 0.0 copy-done.1
  82.0 4.4 %shard_map.50 = (f32[512,1024]{1,0:T(8,128)S(1)}, bf16[768,1024]{1,0:T(8,128)(2,1)S(1)}) custom-call(s32[8,48]{1,0:T(8,128)S(1)} %copy-done.1, bf16[6,2,32,512]{3,2,1,0:T(8,128)(2,1)} %bitcast.3.refs_1_, bf16[6,2,32,512]{3,2,1,0:T(8,128)(2,1)S(1)} %bitcast.10, bf16[6,2,32,512]{3,2,1,0:T(8,128)(2,1)} %shard_map.47.refs_3_, ...), custom_call_target="tpu_custom_call" | custom-call | flops 2415919104 | bytes 9175040 | tf_op jit(solution)/shard_map/pallas_call | solution.py:181
  86.4 0.0 collective-permute-done.4.refs_2_
  86.4 0.0 collective-permute-done.2.refs_1_
  86.4 3.0 %shard_map.51 = bf16[512,1024]{1,0:T(8,128)(2,1)} custom-call(s32[8,48]{1,0:T(8,128)S(1)} %copy-done.1, bf16[6,2,32,512]{3,2,1,0:T(8,128)(2,1)} %collective-permute-done.2.refs_1_, bf16[6,2,32,512]{3,2,1,0:T(8,128)(2,1)} %collective-permute-done.4.refs_2_, bf16[768,1024]{1,0:T(8,128)(2,1)S(1)} %get-tuple-element.7.refs_3_, ...), custom_call_target="tpu_custom_call" | custom-call | flops 805306368 | bytes 4456448 | tf_op jit(solution)/shard_map/pallas_call | solution.py:202
  (4 shorter events, 0.0 us)
Async XLA Ops:
  0.0 15.4 %collective-permute-start = (bf16[32,512]{1,0:T(8,128)(2,1)}, bf16[32,512]{1,0:T(8,128)(2,1)S(1)}, u32[]{:S(2)}, u32[]{:S(2)}) collective-permute-start(bf16[32,512]{1,0:T(8,128)(2,1)} %bitcast.11), channel_id=1, source_target_pairs={{0,48},{1,49},{2,50},{3,51},{4,52},{5,53},{6,54},{7,55},{8,56},{9,... | collective-permute-start | bytes 98312 | tf_op jit(solution)/shard_map/ppermute | solution.py:30
  11.3 4.0 %copy-start = (bf16[512,32]{0,1:T(8,128)(2,1)S(1)}, bf16[512,32]{0,1:T(8,128)(2,1)}, u32[]{:S(2)}) copy-start(bf16[512,32]{0,1:T(8,128)(2,1)} %param.4) | copy-start | bytes 98308
  11.3 55.1 %all-to-all-start = ((bf16[4,384,1024]{2,1,0:T(8,128)(2,1)}), bf16[4,384,1024]{2,1,0:T(8,128)(2,1)S(1)}, u32[]{:S(2)}, u32[]{:S(2)}) async-start(bf16[4,384,1024]{2,1,0:T(8,128)(2,1)} %shard_map.48), calls=%async_computation | async-start | bytes 6291456 | tf_op jit(solution)/shard_map/all_to_all | solution.py:223
  49.4 10.6 %collective-permute-start.3 = (bf16[6,2,32,512]{3,2,1,0:T(8,128)(2,1)S(1)}, bf16[6,2,32,512]{3,2,1,0:T(8,128)(2,1)}, u32[]{:S(2)}, u32[]{:S(2)}) collective-permute-start(bf16[6,2,32,512]{3,2,1,0:T(8,128)(2,1)S(1)} %bitcast.6), channel_id=1, source_target_pairs={{0,84},{1,85},{2,86},{3,87},{4,88},{5,89},{6,90},{7,91},{8,92},{9,... | collective-permute-start | bytes 1179656 | tf_op jit(solution)/shard_map/ppermute | solution.py:30
  51.5 13.0 %collective-permute-start.1 = (bf16[6,2,32,512]{3,2,1,0:T(8,128)(2,1)}, bf16[6,2,32,512]{3,2,1,0:T(8,128)(2,1)}, u32[]{:S(2)}, u32[]{:S(2)}) collective-permute-start(bf16[6,2,32,512]{3,2,1,0:T(8,128)(2,1)} %bitcast.3.refs_1_), channel_id=1, source_target_pairs={{0,12},{1,13},{2,14},{3,15},{4,16},{5,17},{6,18},{7,19},{8,20},{9,... | collective-permute-start | bytes 1179656 | tf_op jit(solution)/shard_map/ppermute | solution.py:30
  54.7 22.0 %collective-permute-start.5 = (bf16[6,2,32,512]{3,2,1,0:T(8,128)(2,1)}, bf16[6,2,32,512]{3,2,1,0:T(8,128)(2,1)}, u32[]{:S(2)}, u32[]{:S(2)}) collective-permute-start(bf16[6,2,32,512]{3,2,1,0:T(8,128)(2,1)} %bitcast.3.refs_1_), channel_id=1, source_target_pairs={{0,84},{1,85},{2,86},{3,87},{4,88},{5,89},{6,90},{7,91},{8,92},{9,... | collective-permute-start | bytes 1179656 | tf_op jit(solution)/shard_map/ppermute | solution.py:30
  58.0 18.7 %collective-permute-start.6 = (bf16[6,2,32,512]{3,2,1,0:T(8,128)(2,1)S(1)}, bf16[6,2,32,512]{3,2,1,0:T(8,128)(2,1)}, u32[]{:S(2)}, u32[]{:S(2)}) collective-permute-start(bf16[6,2,32,512]{3,2,1,0:T(8,128)(2,1)S(1)} %bitcast.7), channel_id=1, source_target_pairs={{0,12},{1,13},{2,14},{3,15},{4,16},{5,17},{6,18},{7,19},{8,20},{9,... | collective-permute-start | bytes 1179656 | tf_op jit(solution)/shard_map/ppermute | solution.py:30
  60.0 26.4 %collective-permute-start.4 = (bf16[6,2,32,512]{3,2,1,0:T(8,128)(2,1)}, bf16[6,2,32,512]{3,2,1,0:T(8,128)(2,1)}, u32[]{:S(2)}, u32[]{:S(2)}) collective-permute-start(bf16[6,2,32,512]{3,2,1,0:T(8,128)(2,1)} %collective-permute-done.3.refs_4_), channel_id=1, source_target_pairs={{0,84},{1,85},{2,86},{3,87},{4,88},{5,89},{6,90},{7,91},{8,92},{9,... | collective-permute-start | bytes 1179656 | tf_op jit(solution)/shard_map/ppermute | solution.py:30
  64.5 21.8 %collective-permute-start.2 = (bf16[6,2,32,512]{3,2,1,0:T(8,128)(2,1)}, bf16[6,2,32,512]{3,2,1,0:T(8,128)(2,1)}, u32[]{:S(2)}, u32[]{:S(2)}) collective-permute-start(bf16[6,2,32,512]{3,2,1,0:T(8,128)(2,1)} %collective-permute-done.1.refs_5_), channel_id=1, source_target_pairs={{0,12},{1,13},{2,14},{3,15},{4,16},{5,17},{6,18},{7,19},{8,20},{9,... | collective-permute-start | bytes 1179656 | tf_op jit(solution)/shard_map/ppermute | solution.py:30
  66.5 15.5 %copy-start.1 = (s32[8,48]{1,0:T(8,128)S(1)}, s32[8,48]{1,0:T(8,128)}, u32[]{:S(2)}) copy-start(s32[8,48]{1,0:T(8,128)} %refs_0_.3) | copy-start | bytes 4612
  66.5 15.5 %collective-permute-start.7 = (bf16[4,384,1024]{2,1,0:T(8,128)(2,1)S(1)}, bf16[4,384,1024]{2,1,0:T(8,128)(2,1)S(1)}, u32[]{:S(2)}, u32[]{:S(2)}) collective-permute-start(bf16[4,384,1024]{2,1,0:T(8,128)(2,1)S(1)} %shard_map.49.refs_7_), channel_id=1, source_target_pairs={{0,96},{96,0},{192,288},{288,192},{384,480},{480,384},{576,672},{6... | collective-permute-start | bytes 9437192 | tf_op jit(solution)/shard_map/ppermute | solution.py:34

commit v4 on v3

--- a/solution.py
+++ b/solution.py
@@ -8,7 +8,10 @@
 TILE = 64
 X, CORES, Y, Z = 4, 2, 8, 12
 FAR, NEAR = 2, 4
-STRIPS = 2
+STRIPS = 4
+PARTS = 3
+WHOLE = pl.BlockSpec(memory_space=pltpu.VMEM)
+HOLD = pl.BlockSpec(memory_space=pl.ANY)
 VMEM_LIMIT = 20 * 1024 * 1024
 HINT = 10**11
 SCREEN_VMEM_LIMIT = 60 * 1024 * 1024
@@ -35,11 +38,10 @@
 
 
 def after(block, other, flops=0):
-    hold = pl.BlockSpec(memory_space=pl.ANY)
     return pl.pallas_call(
         lambda block_ref, other_ref, out_ref: None,
-        in_specs=[hold, hold],
-        out_specs=hold,
+        in_specs=[HOLD, HOLD],
+        out_specs=HOLD,
         out_shape=jax.ShapeDtypeStruct(block.shape, block.dtype),
         input_output_aliases={0: 0},
         compiler_params=pltpu.CompilerParams(vmem_limit_bytes=1024 * 1024),
@@ -47,30 +49,47 @@
     )(block, other)
 
 
-def screen_kernel(mask_ref, block_ref, out_ref, masked, sems):
-    depth, cols = block_ref.shape
-    tiles, tile_cols = mask_ref.shape
+def screen_kernel(mask_ref, block_ref, out_ref, mask, loaded, masked, in_sems, out_sems):
+    depth, cols = loaded.shape
+    tiles, tile_cols = mask.shape
+    copies = out_ref.shape[0]
+    part = depth // PARTS
+    cuts = [pl.ds(p * part, part) for p in range(PARTS)]
+    loads = [pltpu.make_async_copy(mask_ref, mask, in_sems.at[PARTS])]
+    loads += [pltpu.make_async_copy(block_ref.at[cut, :], loaded.at[cut, :], in_sems.at[p]) for p, cut in enumerate(cuts)]
+    for load in loads:
+        load.start()
     across = lax.broadcasted_iota(jnp.int32, (tile_cols, cols), 1) // TILE
     spread_to = (across == lax.broadcasted_iota(jnp.int32, (tile_cols, cols), 0)).astype(jnp.float32)
-    rows = jnp.dot(mask_ref[...].astype(jnp.float32), spread_to, preferred_element_type=jnp.float32).astype(jnp.bfloat16)
-    for t in range(tiles):
-        part = slice(t * TILE, (t + 1) * TILE)
-        masked[part, :] = block_ref[part, :] * rows[t : t + 1, :]
-    copies = [pltpu.make_async_copy(masked, out_ref.at[k], sems.at[k]) for k in range(out_ref.shape[0])]
-    for copy in copies:
-        copy.start()
-    for copy in copies:
-        copy.wait()
+    loads[0].wait()
+    rows = jnp.dot(mask[...].astype(jnp.float32), spread_to, preferred_element_type=jnp.float32).astype(jnp.bfloat16)
+    stores = []
+    for p, cut in enumerate(cuts):
+        loads[p + 1].wait()
+        for t in range(p * tiles // PARTS, (p + 1) * tiles // PARTS):
+            at = slice(t * TILE, (t + 1) * TILE)
+            masked[at, :] = loaded[at, :] * rows[t : t + 1, :]
+        for k in range(copies):
+            sem = out_sems.at[p * copies + k]
+            stores.append(pltpu.make_async_copy(masked.at[cut, :], out_ref.at[k, cut, :], sem))
+            stores[-1].start()
+    for store in stores:
+        store.wait()
 
 
 def screen(block, mask, copies):
-    whole = pl.BlockSpec(memory_space=pltpu.VMEM)
     return pl.pallas_call(
         screen_kernel,
-        in_specs=[whole, whole],
-        out_specs=pl.BlockSpec(memory_space=pl.ANY),
+        in_specs=[HOLD, HOLD],
+        out_specs=HOLD,
         out_shape=jax.ShapeDtypeStruct((copies,) + block.shape, block.dtype),
-        scratch_shapes=[pltpu.VMEM(block.shape, block.dtype), pltpu.SemaphoreType.DMA((copies,))],
+        scratch_shapes=[
+            pltpu.VMEM(mask.shape, mask.dtype),
+            pltpu.VMEM(block.shape, block.dtype),
+            pltpu.VMEM(block.shape, block.dtype),
+            pltpu.SemaphoreType.DMA((PARTS + 1,)),
+            pltpu.SemaphoreType.DMA((PARTS * copies,)),
+        ],
         compiler_params=pltpu.CompilerParams(vmem_limit_bytes=SCREEN_VMEM_LIMIT),
         cost_estimate=pl.CostEstimate(flops=block.size, bytes_accessed=8 * block.size, transcendentals=0),
     )(mask, block)
@@ -118,10 +137,20 @@
         pltpu.make_async_copy(own_ref.at[y // CORES], target, sem).wait()
 
 
-def first_kernel(origins, after_these, mask_ref, *refs):
+def rows_kernel(origins, mask_ref, *refs):
     n = len(origins)
     t_refs, refs = refs[: 2 * n], refs[2 * n :]
-    own_ref, mate_ref, out_ref, later_ref, loaded, lhs, rhs, row_mask, t_sems, v_sems = refs
+    out_ref, loaded, lhs, row_mask, t_sems = refs
+    copies = load_t(t_refs, loaded, t_sems)
+    spread_mask(mask_ref, row_mask)
+    depth = lhs.shape[0]
+    for q, halves in enumerate(origins):
+        screen_t(halves, 0, copies[2 * q : 2 * q + 2], loaded.at[2 * q : 2 * q + 2], row_mask, lhs)
+        out_ref[:, q * depth : (q + 1) * depth] = lhs[...].T
+
+
+def first_kernel(origins, after_these, lhs_ref, own_ref, mate_ref, out_ref, later_ref, rhs, v_sems):
+    n = len(origins)
     cd = own_ref.shape[1]
 
     def fetches(go):
@@ -135,27 +164,24 @@
             sem = v_sems.at[n * FAR + f]
             fetch_v(after_these + NEAR * f, own_ref, mate_ref, later_ref.at[pl.ds(f * cd, cd), :], sem, go)
 
-    copies = load_t(t_refs, loaded, t_sems)
     fetches(True)
     later(True)
-    spread_mask(mask_ref, row_mask)
-    for q, halves in enumerate(origins):
-        screen_t(halves, q, copies, loaded, row_mask, lhs)
     fetches(False)
-    out_ref[...] = lax.dot_general(lhs[...], rhs[...], (((0,), (0,)), ((), ())), preferred_element_type=jnp.float32)
+    out_ref[...] = jnp.dot(lhs_ref[...], rhs[...], preferred_element_type=jnp.float32)
     later(False)
 
 
-def last_kernel(halves, mask_ref, a_ref, b_ref, v_ref, acc_ref, out_ref, loaded, lhs, row_mask, block, t_sems, out_sems):
+def last_kernel(halves, mask_ref, a_ref, b_ref, v_ref, acc_ref, out_ref, loaded, rows, lhs, row_mask, block, t_sems, out_sems):
     copies = load_t((a_ref, b_ref), loaded, t_sems)
     spread_mask(mask_ref, row_mask)
-    screen_t(halves, 0, copies, loaded, row_mask, lhs)
+    screen_t(halves, 0, copies, loaded, row_mask, rows)
+    lhs[...] = rows[...].T
     strips = block.shape[0]
     wide = block.shape[2]
     stores = []
     for s in range(strips):
         columns = slice(s * wide, (s + 1) * wide)
-        total = lax.dot_general(lhs[...], v_ref[:, columns], (((0,), (0,)), ((), ())), preferred_element_type=jnp.float32)
+        total = jnp.dot(lhs[...], v_ref[:, columns], preferred_element_type=jnp.float32)
         block[s] = (total + acc_ref[:, columns]).astype(block.dtype)
         stores.append(pltpu.make_async_copy(block.at[s], out_ref.at[:, pl.ds(s * wide, wide)], out_sems.at[s]))
         stores[-1].start()
@@ -163,37 +189,45 @@
         store.wait()
 
 
-WHOLE = pl.BlockSpec(memory_space=pltpu.VMEM)
-HOLD = pl.BlockSpec(memory_space=pl.ANY)
-
-
 def hint(rows, cols, depth):
     return pl.CostEstimate(
         flops=2 * rows * cols * depth, bytes_accessed=2 * depth * (rows + cols) + 4 * rows * cols, transcendentals=0
     )
 
 
-def first_product(origins, after_these, ts, amp_mask, v_own, v_mate):
-    n = len(origins)
-    rows = ts[0].shape[-1]
-    cd, cols = v_own.shape[1:]
-    depth = n * FAR * cd
-    return pl.pallas_call(
-        lambda *refs: first_kernel(origins, after_these, *refs),
-        in_specs=[WHOLE] + [HOLD] * (2 * n + 2),
-        out_specs=(WHOLE, WHOLE),
-        out_shape=(jax.ShapeDtypeStruct((rows, cols), jnp.float32), jax.ShapeDtypeStruct((FAR * cd, cols), v_own.dtype)),
+def masked_rows(origins, ts, amp_mask):
+    n = len(origins)
+    some, far, r, rows = ts[0].shape
+    depth = 2 * some * far * r
+    return pl.pallas_call(
+        lambda *refs: rows_kernel(origins, *refs),
+        in_specs=[WHOLE] + [HOLD] * (2 * n),
+        out_specs=WHOLE,
+        out_shape=jax.ShapeDtypeStruct((rows, n * depth), jnp.bfloat16),
         scratch_shapes=[
             pltpu.VMEM((2 * n,) + ts[0].shape, jnp.bfloat16),
             pltpu.VMEM((depth, rows), jnp.bfloat16),
-            pltpu.VMEM((depth, cols), jnp.bfloat16),
             pltpu.VMEM((amp_mask.shape[1], rows), jnp.float32),
             pltpu.SemaphoreType.DMA((2 * n,)),
-            pltpu.SemaphoreType.DMA(((n + 1) * FAR,)),
         ],
         compiler_params=pltpu.CompilerParams(vmem_limit_bytes=VMEM_LIMIT),
+        cost_estimate=pl.CostEstimate(flops=rows * n * depth, bytes_accessed=4 * rows * n * depth, transcendentals=0),
+    )(amp_mask, *ts)
+
+
+def first_product(origins, after_these, lhs, v_own, v_mate):
+    n = len(origins)
+    rows, depth = lhs.shape
+    cd, cols = v_own.shape[1:]
+    return pl.pallas_call(
+        lambda *refs: first_kernel(origins, after_these, *refs),
+        in_specs=[WHOLE, HOLD, HOLD],
+        out_specs=(WHOLE, WHOLE),
+        out_shape=(jax.ShapeDtypeStruct((rows, cols), jnp.float32), jax.ShapeDtypeStruct((FAR * cd, cols), v_own.dtype)),
+        scratch_shapes=[pltpu.VMEM((depth, cols), jnp.bfloat16), pltpu.SemaphoreType.DMA(((n + 1) * FAR,))],
+        compiler_params=pltpu.CompilerParams(vmem_limit_bytes=VMEM_LIMIT),
         cost_estimate=hint(rows, cols, depth),
-    )(amp_mask, *ts, v_own, v_mate)
+    )(lhs, v_own, v_mate)
 
 
 def last_product(halves, t_a, t_b, amp_mask, v, acc):
@@ -207,6 +241,7 @@
         scratch_shapes=[
             pltpu.VMEM((2,) + t_a.shape, jnp.bfloat16),
             pltpu.VMEM((depth, rows), jnp.bfloat16),
+            pltpu.VMEM((rows, depth), jnp.bfloat16),
             pltpu.VMEM((amp_mask.shape[1], rows), jnp.float32),
             pltpu.VMEM((STRIPS, rows, cols // STRIPS), jnp.bfloat16),
             pltpu.SemaphoreType.DMA((2,)),
@@ -234,7 +269,8 @@
     two_b = shift_y(above_b, -1)
 
     ts = (w_a, w_b, above_a, above_b, below_a, below_b)
-    acc, v_two = first_product(((0, 0), (1, 1), (Y - 1, Y - 1)), Y - 2, ts, amp_mask, v_own, v_mate)
+    origins = ((0, 0), (1, 1), (Y - 1, Y - 1))
+    acc, v_two = first_product(origins, Y - 2, masked_rows(origins, ts, amp_mask), v_own, v_mate)
     return last_product((Y - 2, 2), two_a, two_b, amp_mask, v_two, acc)
 
 

time: 89.9 us -> 89.4 us (level)
  waiting for transfers between devices: 5.25 us -> 3.3 us
  starting transfers between devices: 39.5 us -> 40.4 us
    ppermute x1, waiting for transfers between devices: 5.23 us -> 3.28 us  [swap_cores(): lax.ppermute(block, 'occ', [(occ(x, c), occ(x, 1 - c)) for x in range(X)...]
    pallas_call x4 -> x5, Pallas kernels: 3.03 us -> 4.7 us  [the longest x1 2.75 us: screen(): pl.pallas_call(screen_kernel, in_specs=[HOLD, HOLD], out_specs=HOLD, out_...]
    ppermute x7, starting transfers between devices: 25.3 us -> 26.5 us  [shift_y(): lax.ppermute(block, 'vir', [(vir(y, z), vir(y + step, z)) for y in range(...]
    pallas_call x1, Pallas kernels: 4.36 us -> 3.25 us  [first_product(): pl.pallas_call(lambda *refs: first_kernel(origins, after_these, *refs), i...]
  transfers between devices with their start and end apart: 9 -> 9, of which waited for: 1 -> 1; matrix products, arithmetic and copies ran while one was open for 1% -> 1% of each run, Pallas kernels for 8% -> 9%
where the time goes in v4:
time: 89.4 us; the launch traced here: 88.9 us
  starting transfers between devices  40.4 us (45%)
  blocking collectives  33.2 us (37%)
  Pallas kernels  10.9 us (12%)
  waiting for transfers between devices  3.3 us (4%)
    all_gather x1, blocking collectives, on_device(): lax.all_gather(jnp.stack([t, other]), 'vir', axis=0, axis_index_groups=Z_...  33.2 us
    ppermute x7, starting transfers between devices, shift_y(): lax.ppermute(block, 'vir', [(vir(y, z), vir(y + step, z)) for y in range(...  26.5 us
    ppermute x1, starting transfers between devices, swap_cores(): lax.ppermute(block, 'occ', [(occ(x, c), occ(x, 1 - c)) for x in range(X)...  9.82 us
    all_to_all x1, starting transfers between devices, on_device(): lax.all_to_all(screen(integrals, int_mask, X), 'occ', 0, 0, axis_index_gr...  4.02 us
    ppermute x1, waiting for transfers between devices, swap_cores(): lax.ppermute(block, 'occ', [(occ(x, c), occ(x, 1 - c)) for x in range(X)...  3.28 us
    pallas_call x1, Pallas kernels, first_product(): pl.pallas_call(lambda *refs: first_kernel(origins, after_these, *refs), i...  3.25 us
    pallas_call x1, Pallas kernels, last_product(): pl.pallas_call(lambda *refs: last_kernel(halves, *refs), in_specs=[WHOLE,...  3 us
    pallas_call x1, Pallas kernels, screen(): pl.pallas_call(screen_kernel, in_specs=[HOLD, HOLD], out_specs=HOLD, out_...  2.75 us
  transfers between devices with their start and end apart: 9, of which 1 were waited for; matrix products, arithmetic and copies ran while one was open for 1% of the time, Pallas kernels for 9%

profile of v4, /device:TPU:1, one launch (start us, length us, event | category | flops | bytes accessed | tf_op | source)
XLA Modules:
  0.0 88.9 jit_solution(4136906694053058660)
XLA Ops:
  0.0 8.3 %collective-permute-start = (bf16[32,512]{1,0:T(8,128)(2,1)}, bf16[32,512]{1,0:T(8,128)(2,1)S(1)}, u32[]{:S(2)}, u32[]{:S(2)}) collective-permute-start(bf16[32,512]{1,0:T(8,128)(2,1)} %bitcast.11), channel_id=1, source_target_pairs={{0,48},{1,49},{2,50},{3,51},{4,52},{5,53},{6,54},{7,55},{8,56},{9,... | collective-permute-start | bytes 98312 | tf_op jit(solution)/shard_map/ppermute | solution.py:33
  8.3 2.8 %shard_map.49 = bf16[4,384,1024]{2,1,0:T(8,128)(2,1)} custom-call(s32[6,16]{1,0:T(8,128)} %mask_ref.1, bf16[384,1024]{1,0:T(8,128)(2,1)} %block_ref.1), custom_call_target="tpu_custom_call" | custom-call | flops 393216 | bytes 3145728 | tf_op jit(solution)/shard_map/pallas_call | solution.py:81
  11.0 0.0 copy-start
  11.1 4.0 %all-to-all-start = ((bf16[4,384,1024]{2,1,0:T(8,128)(2,1)}), bf16[4,384,1024]{2,1,0:T(8,128)(2,1)S(1)}, u32[]{:S(2)}, u32[]{:S(2)}) async-start(bf16[4,384,1024]{2,1,0:T(8,128)(2,1)} %shard_map.49), calls=%async_computation | async-start | bytes 6291456 | tf_op jit(solution)/shard_map/all_to_all | solution.py:258
  15.1 0.0 collective-permute-done.block_ref
  15.1 0.0 copy-done
  15.1 33.2 %all-gather = bf16[24,32,512]{2,1,0:T(8,128)(2,1)S(1)} all-gather(bf16[2,32,512]{2,1,0:T(8,128)(2,1)S(1)} %pad_maximum_fusion), channel_id=2, replica_groups={{0,1,2,3,4,5,6,7,8,9,10,11},{12,13,14,15,16,17,18,19,20,21,22,23},{24,2..., dimensions={0}, use_global_device_ids=true | all-gather | bytes 851968 | tf_op jit(solution)/shard_map/all_gather | solution.py:260
  48.3 0.8 fusion
  49.1 2.3 %collective-permute-start.1 = (bf16[6,2,32,512]{3,2,1,0:T(8,128)(2,1)}, bf16[6,2,32,512]{3,2,1,0:T(8,128)(2,1)}, u32[]{:S(2)}, u32[]{:S(2)}) collective-permute-start(bf16[6,2,32,512]{3,2,1,0:T(8,128)(2,1)} %bitcast.3.refs_1_), channel_id=1, source_target_pairs={{0,12},{1,13},{2,14},{3,15},{4,16},{5,17},{6,18},{7,19},{8,20},{9,... | collective-permute-start | bytes 1179656 | tf_op jit(solution)/shard_map/ppermute | solution.py:33
  51.4 4.2 %collective-permute-start.3 = (bf16[6,2,32,512]{3,2,1,0:T(8,128)(2,1)S(1)}, bf16[6,2,32,512]{3,2,1,0:T(8,128)(2,1)}, u32[]{:S(2)}, u32[]{:S(2)}) collective-permute-start(bf16[6,2,32,512]{3,2,1,0:T(8,128)(2,1)S(1)} %bitcast.6), channel_id=1, source_target_pairs={{0,84},{1,85},{2,86},{3,87},{4,88},{5,89},{6,90},{7,91},{8,92},{9,... | collective-permute-start | bytes 1179656 | tf_op jit(solution)/shard_map/ppermute | solution.py:33
  55.6 1.9 %collective-permute-start.5 = (bf16[6,2,32,512]{3,2,1,0:T(8,128)(2,1)}, bf16[6,2,32,512]{3,2,1,0:T(8,128)(2,1)}, u32[]{:S(2)}, u32[]{:S(2)}) collective-permute-start(bf16[6,2,32,512]{3,2,1,0:T(8,128)(2,1)} %bitcast.3.refs_1_), channel_id=1, source_target_pairs={{0,84},{1,85},{2,86},{3,87},{4,88},{5,89},{6,90},{7,91},{8,92},{9,... | collective-permute-start | bytes 1179656 | tf_op jit(solution)/shard_map/ppermute | solution.py:33
  57.6 3.4 %collective-permute-start.6 = (bf16[6,2,32,512]{3,2,1,0:T(8,128)(2,1)S(1)}, bf16[6,2,32,512]{3,2,1,0:T(8,128)(2,1)}, u32[]{:S(2)}, u32[]{:S(2)}) collective-permute-start(bf16[6,2,32,512]{3,2,1,0:T(8,128)(2,1)S(1)} %bitcast.7), channel_id=1, source_target_pairs={{0,12},{1,13},{2,14},{3,15},{4,16},{5,17},{6,18},{7,19},{8,20},{9,... | collective-permute-start | bytes 1179656 | tf_op jit(solution)/shard_map/ppermute | solution.py:33
  60.9 0.0 collective-permute-done.1.refs_5_
  60.9 1.9 %collective-permute-start.2 = (bf16[6,2,32,512]{3,2,1,0:T(8,128)(2,1)}, bf16[6,2,32,512]{3,2,1,0:T(8,128)(2,1)}, u32[]{:S(2)}, u32[]{:S(2)}) collective-permute-start(bf16[6,2,32,512]{3,2,1,0:T(8,128)(2,1)} %collective-permute-done.1.refs_5_), channel_id=1, source_target_pairs={{0,12},{1,13},{2,14},{3,15},{4,16},{5,17},{6,18},{7,19},{8,20},{9,... | collective-permute-start | bytes 1179656 | tf_op jit(solution)/shard_map/ppermute | solution.py:33
  62.9 0.0 collective-permute-done.3.refs_4_
  62.9 4.6 %collective-permute-start.4 = (bf16[6,2,32,512]{3,2,1,0:T(8,128)(2,1)}, bf16[6,2,32,512]{3,2,1,0:T(8,128)(2,1)}, u32[]{:S(2)}, u32[]{:S(2)}) collective-permute-start(bf16[6,2,32,512]{3,2,1,0:T(8,128)(2,1)} %collective-permute-done.3.refs_4_), channel_id=1, source_target_pairs={{0,84},{1,85},{2,86},{3,87},{4,88},{5,89},{6,90},{7,91},{8,92},{9,... | collective-permute-start | bytes 1179656 | tf_op jit(solution)/shard_map/ppermute | solution.py:33
  67.5 0.0 all-to-all-done.block_ref
  67.5 0.0 copy-start.1
  67.5 9.8 %collective-permute-start.7 = (bf16[4,384,1024]{2,1,0:T(8,128)(2,1)S(1)}, bf16[4,384,1024]{2,1,0:T(8,128)(2,1)S(1)}, u32[]{:S(2)}, u32[]{:S(2)}) collective-permute-start(bf16[4,384,1024]{2,1,0:T(8,128)(2,1)S(1)} %shard_map.50.refs_1_), channel_id=1, source_target_pairs={{0,96},{96,0},{192,288},{288,192},{384,480},{480,384},{576,672},{6... | collective-permute-start | bytes 9437192 | tf_op jit(solution)/shard_map/ppermute | solution.py:37
  77.3 0.0 collective-permute-done.5.block_ref
  77.4 0.0 collective-permute-done.6.refs_6_
  77.4 0.0 copy-done.1
  77.4 1.9 %shard_map.48.refs_0_ = bf16[512,2304]{1,0:T(8,128)(2,1)S(1)} custom-call(s32[8,48]{1,0:T(8,128)S(1)} %copy-done.1, bf16[6,2,32,512]{3,2,1,0:T(8,128)(2,1)} %bitcast.3.refs_1_, bf16[6,2,32,512]{3,2,1,0:T(8,128)(2,1)S(1)} %bitcast.10, bf16[6,2,32,512]{3,2,1,0:T(8,128)(2,1)} %shard_map.47.refs_3_, bf16[6,2,32,512]{3,2,1,0:T(8,128)(2,1)} %collective-permute-done.3.refs_4_, ...), custom_call_target="tpu_custom_call" | custom-call | flops 1179648 | bytes 4718592 | tf_op jit(solution)/shard_map/pallas_call | solution.py:202
  79.3 3.3 %collective-permute-done.7.refs_2_ = bf16[4,384,1024]{2,1,0:T(8,128)(2,1)S(1)} collective-permute-done((bf16[4,384,1024]{2,1,0:T(8,128)(2,1)S(1)}, bf16[4,384,1024]{2,1,0:T(8,128)(2,1)S(1)}, u32[]{:S(2)}, u32[]{:S(2)}) %collective-permute-start.7) | collective-permute-done | bytes 3145760 | tf_op jit(solution)/shard_map/ppermute | solution.py:37
  82.6 3.2 %shard_map.51 = (f32[512,1024]{1,0:T(8,128)S(1)}, bf16[768,1024]{1,0:T(8,128)(2,1)S(1)}) custom-call(bf16[512,2304]{1,0:T(8,128)(2,1)S(1)} %shard_map.48.refs_0_, bf16[4,384,1024]{2,1,0:T(8,128)(2,1)S(1)} %shard_map.50.refs_1_, bf16[4,384,1024]{2,1,0:T(8,128)(2,1)S(1)} %collective-permute-done.7.refs_2_), custom_call_target="tpu_custom_call" | custom-call | flops 2415919104 | bytes 9175040 | tf_op jit(solution)/shard_map/pallas_call | solution.py:222
  85.9 0.0 collective-permute-done.2.refs_1_
  85.9 0.0 collective-permute-done.4.refs_2_
  85.9 3.0 %shard_map.52 = bf16[512,1024]{1,0:T(8,128)(2,1)} custom-call(s32[8,48]{1,0:T(8,128)S(1)} %copy-done.1, bf16[6,2,32,512]{3,2,1,0:T(8,128)(2,1)} %collective-permute-done.2.refs_1_, bf16[6,2,32,512]{3,2,1,0:T(8,128)(2,1)} %collective-permute-done.4.refs_2_, bf16[768,1024]{1,0:T(8,128)(2,1)S(1)} %get-tuple-element.7.refs_3_, ...), custom_call_target="tpu_custom_call" | custom-call | flops 805306368 | bytes 4456448 | tf_op jit(solution)/shard_map/pallas_call | solution.py:236
  (4 shorter events, 0.0 us)
Async XLA Ops:
  0.0 15.1 %collective-permute-start = (bf16[32,512]{1,0:T(8,128)(2,1)}, bf16[32,512]{1,0:T(8,128)(2,1)S(1)}, u32[]{:S(2)}, u32[]{:S(2)}) collective-permute-start(bf16[32,512]{1,0:T(8,128)(2,1)} %bitcast.11), channel_id=1, source_target_pairs={{0,48},{1,49},{2,50},{3,51},{4,52},{5,53},{6,54},{7,55},{8,56},{9,... | collective-permute-start | bytes 98312 | tf_op jit(solution)/shard_map/ppermute | solution.py:33
  11.0 4.0 %copy-start = (bf16[512,32]{0,1:T(8,128)(2,1)S(1)}, bf16[512,32]{0,1:T(8,128)(2,1)}, u32[]{:S(2)}) copy-start(bf16[512,32]{0,1:T(8,128)(2,1)} %param.4) | copy-start | bytes 98308
  11.1 56.4 %all-to-all-start = ((bf16[4,384,1024]{2,1,0:T(8,128)(2,1)}), bf16[4,384,1024]{2,1,0:T(8,128)(2,1)S(1)}, u32[]{:S(2)}, u32[]{:S(2)}) async-start(bf16[4,384,1024]{2,1,0:T(8,128)(2,1)} %shard_map.49), calls=%async_computation | async-start | bytes 6291456 | tf_op jit(solution)/shard_map/all_to_all | solution.py:258
  49.1 11.8 %collective-permute-start.1 = (bf16[6,2,32,512]{3,2,1,0:T(8,128)(2,1)}, bf16[6,2,32,512]{3,2,1,0:T(8,128)(2,1)}, u32[]{:S(2)}, u32[]{:S(2)}) collective-permute-start(bf16[6,2,32,512]{3,2,1,0:T(8,128)(2,1)} %bitcast.3.refs_1_), channel_id=1, source_target_pairs={{0,12},{1,13},{2,14},{3,15},{4,16},{5,17},{6,18},{7,19},{8,20},{9,... | collective-permute-start | bytes 1179656 | tf_op jit(solution)/shard_map/ppermute | solution.py:33
  51.4 11.4 %collective-permute-start.3 = (bf16[6,2,32,512]{3,2,1,0:T(8,128)(2,1)S(1)}, bf16[6,2,32,512]{3,2,1,0:T(8,128)(2,1)}, u32[]{:S(2)}, u32[]{:S(2)}) collective-permute-start(bf16[6,2,32,512]{3,2,1,0:T(8,128)(2,1)S(1)} %bitcast.6), channel_id=1, source_target_pairs={{0,84},{1,85},{2,86},{3,87},{4,88},{5,89},{6,90},{7,91},{8,92},{9,... | collective-permute-start | bytes 1179656 | tf_op jit(solution)/shard_map/ppermute | solution.py:33
  55.6 21.7 %collective-permute-start.5 = (bf16[6,2,32,512]{3,2,1,0:T(8,128)(2,1)}, bf16[6,2,32,512]{3,2,1,0:T(8,128)(2,1)}, u32[]{:S(2)}, u32[]{:S(2)}) collective-permute-start(bf16[6,2,32,512]{3,2,1,0:T(8,128)(2,1)} %bitcast.3.refs_1_), channel_id=1, source_target_pairs={{0,84},{1,85},{2,86},{3,87},{4,88},{5,89},{6,90},{7,91},{8,92},{9,... | collective-permute-start | bytes 1179656 | tf_op jit(solution)/shard_map/ppermute | solution.py:33
  57.6 19.8 %collective-permute-start.6 = (bf16[6,2,32,512]{3,2,1,0:T(8,128)(2,1)S(1)}, bf16[6,2,32,512]{3,2,1,0:T(8,128)(2,1)}, u32[]{:S(2)}, u32[]{:S(2)}) collective-permute-start(bf16[6,2,32,512]{3,2,1,0:T(8,128)(2,1)S(1)} %bitcast.7), channel_id=1, source_target_pairs={{0,12},{1,13},{2,14},{3,15},{4,16},{5,17},{6,18},{7,19},{8,20},{9,... | collective-permute-start | bytes 1179656 | tf_op jit(solution)/shard_map/ppermute | solution.py:33
  60.9 24.9 %collective-permute-start.2 = (bf16[6,2,32,512]{3,2,1,0:T(8,128)(2,1)}, bf16[6,2,32,512]{3,2,1,0:T(8,128)(2,1)}, u32[]{:S(2)}, u32[]{:S(2)}) collective-permute-start(bf16[6,2,32,512]{3,2,1,0:T(8,128)(2,1)} %collective-permute-done.1.refs_5_), channel_id=1, source_target_pairs={{0,12},{1,13},{2,14},{3,15},{4,16},{5,17},{6,18},{7,19},{8,20},{9,... | collective-permute-start | bytes 1179656 | tf_op jit(solution)/shard_map/ppermute | solution.py:33
  62.9 23.0 %collective-permute-start.4 = (bf16[6,2,32,512]{3,2,1,0:T(8,128)(2,1)}, bf16[6,2,32,512]{3,2,1,0:T(8,128)(2,1)}, u32[]{:S(2)}, u32[]{:S(2)}) collective-permute-start(bf16[6,2,32,512]{3,2,1,0:T(8,128)(2,1)} %collective-permute-done.3.refs_4_), channel_id=1, source_target_pairs={{0,84},{1,85},{2,86},{3,87},{4,88},{5,89},{6,90},{7,91},{8,92},{9,... | collective-permute-start | bytes 1179656 | tf_op jit(solution)/shard_map/ppermute | solution.py:33
  67.5 9.9 %copy-start.1 = (s32[8,48]{1,0:T(8,128)S(1)}, s32[8,48]{1,0:T(8,128)}, u32[]{:S(2)}) copy-start(s32[8,48]{1,0:T(8,128)} %refs_0_.3) | copy-start | bytes 4612
  67.5 15.1 %collective-permute-start.7 = (bf16[4,384,1024]{2,1,0:T(8,128)(2,1)S(1)}, bf16[4,384,1024]{2,1,0:T(8,128)(2,1)S(1)}, u32[]{:S(2)}, u32[]{:S(2)}) collective-permute-start(bf16[4,384,1024]{2,1,0:T(8,128)(2,1)S(1)} %shard_map.50.refs_1_), channel_id=1, source_target_pairs={{0,96},{96,0},{192,288},{288,192},{384,480},{480,384},{576,672},{6... | collective-permute-start | bytes 9437192 | tf_op jit(solution)/shard_map/ppermute | solution.py:37
